TPU v7x, 256 devices: a whole 4x4x8 slice. The times are simulated.
256 devices in a mesh: src: 32 (over x, z), tgt: 8 (over y, core).
Axes of the slice: x: 4, y: 4, z: 8, core: 2. Of those that a mesh axis runs over, the one named last changes fastest.
Arguments:
- src_points: float32 [64, 16384], P(None, 'src'), may hold values from -0.43 to 0.43
- tgt_points: float32 [64, 32768], P(None, 'tgt'), may hold values from -0.43 to 0.43
- src_potential: float32 [16384], P('src'), may hold values from -1 to 1
- tgt_potential: float32 [32768], P('tgt'), may hold values from -1 to 1
- src_rhs: float32 [16384], P('src'), may hold values from -16 to 16
- tgt_rhs: float32 [32768], P('tgt'), may hold values from -16 to 16
Outputs:
- sol_src: float32 [16384], P('src')
- sol_tgt: float32 [32768], P('tgt')
- grad_src: float32 [64, 16384], P(None, 'src')
- grad_tgt: float32 [64, 32768], P(None, 'tgt')
All inputs are finite; a program needn't handle non-finite values.
Results may differ from a plain program's by a relative error of at most 0.0001.
Values sent between devices are 32-bit elements; how exact they have to be, the bound alone decides.
A program may use at most 64 MiB of HBM per device.

v0:
```python
import math

import jax
import jax.numpy as jnp
from jax import lax
from jax.sharding import PartitionSpec as P

ITERS = 3


EPSILON = 0.5
REGULARIZER = 1.0
HIGHEST = lax.Precision.HIGHEST


def body(src_points, tgt_points, src_potential, tgt_potential, src_rhs, tgt_rhs):
    src_ways = lax.axis_size("src")
    tgt_ways = lax.axis_size("tgt")
    normalizer = 1.0 / math.sqrt(src_points.shape[1] * src_ways * (tgt_points.shape[1] * tgt_ways))

    def build_plan():
        cross_term = jnp.dot(
            src_points.T, tgt_points, precision=HIGHEST, preferred_element_type=jnp.float32
        )
        return (
            jnp.exp(cross_term / EPSILON + src_potential[:, None] + tgt_potential[None, :])
            * normalizer
        )

    def fetch_plan():
        return build_plan()

    plan_block = fetch_plan()
    mass_src = lax.psum(jnp.sum(plan_block, axis=1), "tgt")
    mass_tgt = lax.psum(jnp.sum(plan_block, axis=0), "src")

    def inner_product(a_src, a_tgt, b_src, b_tgt):
        local_term = jnp.sum(a_src * b_src) / tgt_ways + jnp.sum(a_tgt * b_tgt) / src_ways
        return lax.psum(local_term, ("src", "tgt"))

    sol_src = jnp.zeros_like(src_rhs)
    sol_tgt = jnp.zeros_like(tgt_rhs)
    res_src, res_tgt = (src_rhs, tgt_rhs)
    dir_src, dir_tgt = (src_rhs, tgt_rhs)
    norm_now = inner_product(res_src, res_tgt, res_src, res_tgt)
    for repeat in range(ITERS):
        plan_now = fetch_plan()
        row_out = lax.psum(jnp.dot(plan_now, dir_tgt, precision=HIGHEST), "tgt")
        col_out = lax.psum(jnp.dot(dir_src, plan_now, precision=HIGHEST), "src")
        img_src = (mass_src + REGULARIZER) * dir_src + row_out
        img_tgt = (mass_tgt + REGULARIZER) * dir_tgt + col_out
        step_size = norm_now / inner_product(dir_src, dir_tgt, img_src, img_tgt)
        sol_src = sol_src + step_size * dir_src
        sol_tgt = sol_tgt + step_size * dir_tgt
        res_src = res_src - step_size * img_src
        res_tgt = res_tgt - step_size * img_tgt
        norm_next = inner_product(res_src, res_tgt, res_src, res_tgt)
        direction_ratio = norm_next / norm_now
        dir_src = res_src + direction_ratio * dir_src
        dir_tgt = res_tgt + direction_ratio * dir_tgt
        norm_now = norm_next
    weight = fetch_plan() * (1.0 + sol_src[:, None] + sol_tgt[None, :])
    row_weight = jnp.sum(weight, axis=1)
    weighted_y = lax.dot_general(tgt_points, weight, (((1,), (1,)), ((), ())), precision=HIGHEST)
    row_weight, weighted_y = lax.psum((row_weight, weighted_y), "tgt")
    grad_src = (row_weight[None, :] * src_points - weighted_y) / EPSILON
    col_weight = jnp.sum(weight, axis=0)
    weighted_x = jnp.dot(src_points, weight, precision=HIGHEST)
    col_weight, weighted_x = lax.psum((col_weight, weighted_x), "src")
    grad_tgt = (col_weight[None, :] * tgt_points - weighted_x) / EPSILON
    return (sol_src, sol_tgt, grad_src, grad_tgt)


def solution(mesh):
    return jax.shard_map(
        body,
        mesh=mesh,
        in_specs=(P(None, "src"), P(None, "tgt"), P("src"), P("tgt"), P("src"), P("tgt")),
        out_specs=(P("src"), P("tgt"), P(None, "src"), P(None, "tgt")),
        check_vma=False,
    )
```

profile of v0, /device:TPU:1, one launch (start us, length us, event | category | flops | bytes accessed | tf_op | source)
XLA Modules:
  0.0 1142.7 jit_solution(15714931214253614030)
XLA Ops:
  7.2 9.9 fusion.10
  17.1 7.6 fusion.11
  24.8 4.5 fusion.12
  29.2 15.0 %all-reduce.2 = (f32[512]{0:T(512)S(1)}, f32[512]{0:T(512)S(1)}) all-reduce(f32[512]{0:T(512)S(1)} %bitcast.41, f32[512]{0:T(512)S(1)} %get-tuple-element.7), channel_id=1, replica_groups=mesh['src'=32,'tgt'=8] {'tgt'}, use_global_device_ids=true, to_apply=%region_5.0 | all-reduce | flops 1024 | bytes 8192 | tf_op jit(solution)/shard_map/psum | solution.py:48
  46.2 116.0 %all-reduce.1 = (f32[4096]{0:T(1024)S(1)}, f32[4096]{0:T(1024)S(1)}) all-reduce(f32[4096]{0:T(1024)S(1)} %bitcast.36, f32[4096]{0:T(1024)S(1)} %get-tuple-element.6), channel_id=1, replica_groups=mesh['src'=32,'tgt'=8] {'src'}, use_global_device_ids=true, to_apply=%region_9.0 | all-reduce | flops 8192 | bytes 65536 | tf_op jit(solution)/shard_map/psum | solution.py:49
  164.1 101.5 %all-reduce = (f32[]{:T(128)}, f32[]{:T(128)}) all-reduce(f32[]{:T(128)S(6)} %add.60, f32[]{:T(128)S(6)} %add.102), channel_id=1, replica_groups=mesh['src'=32,'tgt'=8] {'src','tgt'}, use_global_device_ids=true, to_apply=%region_2.0 | all-reduce | flops 2 | bytes 16 | tf_op jit(solution)/shard_map/psum | solution.py:39
  269.5 74.4 %psum.132 = f32[]{:T(128)} all-reduce(f32[]{:T(128)S(6)} %add.103), channel_id=1, replica_groups=mesh['src'=32,'tgt'=8] {'src','tgt'}, use_global_device_ids=true, to_apply=%region_14.0 | all-reduce | flops 1 | bytes 8 | tf_op jit(solution)/shard_map/psum | solution.py:39
  345.2 6.3 fusion.14
  351.6 113.2 %psum.134 = f32[4096]{0:T(1024)S(1)} all-reduce(f32[4096]{0:T(1024)S(1)} %bitcast.37), channel_id=1, replica_groups=mesh['src'=32,'tgt'=8] {'src'}, use_global_device_ids=true, to_apply=%region_17.0 | all-reduce | flops 4096 | bytes 32768 | tf_op jit(solution)/shard_map/psum | solution.py:49
  465.4 9.4 fusion.13
  474.8 40.3 %psum.133 = f32[512]{0:T(512)S(1)} all-reduce(f32[512]{0:T(512)S(1)} %bitcast.42), channel_id=1, replica_groups=mesh['src'=32,'tgt'=8] {'tgt'}, use_global_device_ids=true, to_apply=%region_15.0 | all-reduce | flops 512 | bytes 4096 | tf_op jit(solution)/shard_map/psum | solution.py:48
  517.0 72.6 %psum.135 = f32[]{:T(128)} all-reduce(f32[]{:T(128)S(6)} %add.187), channel_id=1, replica_groups=mesh['src'=32,'tgt'=8] {'src','tgt'}, use_global_device_ids=true, to_apply=%region_19.0 | all-reduce | flops 1 | bytes 8 | tf_op jit(solution)/shard_map/psum | solution.py:39
  593.4 73.5 %psum.136 = f32[]{:T(128)} all-reduce(f32[]{:T(128)S(6)} %add.189), channel_id=1, replica_groups=mesh['src'=32,'tgt'=8] {'src','tgt'}, use_global_device_ids=true, to_apply=%region_22.0 | all-reduce | flops 1 | bytes 8 | tf_op jit(solution)/shard_map/psum | solution.py:39
  668.3 6.4 fusion.16
  674.7 112.4 %psum.138 = f32[4096]{0:T(1024)S(1)} all-reduce(f32[4096]{0:T(1024)S(1)} %bitcast.38), channel_id=1, replica_groups=mesh['src'=32,'tgt'=8] {'src'}, use_global_device_ids=true, to_apply=%region_25.0 | all-reduce | flops 4096 | bytes 32768 | tf_op jit(solution)/shard_map/psum | solution.py:49
  787.7 9.5 fusion.15
  797.2 40.3 %psum.137 = f32[512]{0:T(512)S(1)} all-reduce(f32[512]{0:T(512)S(1)} %bitcast.43), channel_id=1, replica_groups=mesh['src'=32,'tgt'=8] {'tgt'}, use_global_device_ids=true, to_apply=%region_23.0 | all-reduce | flops 512 | bytes 4096 | tf_op jit(solution)/shard_map/psum | solution.py:48
  839.4 72.8 %psum.139 = f32[]{:T(128)} all-reduce(f32[]{:T(128)S(6)} %add.194), channel_id=1, replica_groups=mesh['src'=32,'tgt'=8] {'src','tgt'}, use_global_device_ids=true, to_apply=%region_27.0 | all-reduce | flops 1 | bytes 8 | tf_op jit(solution)/shard_map/psum | solution.py:39
  914.2 11.8 %fusion.9 = f32[64,512]{1,0:T(8,128)} fusion(f32[64,4096]{1,0:T(8,128)S(1)} %copy-done.1, f32[512,4096]{1,0:T(8,128)} %copy-done, f32[4096]{0:T(1024)S(1)} %multiply_add_fusion, f32[512]{0:T(512)S(1)} %get-tuple-element.18), kind=kOutput, calls=%fused_computation.11 | convolution fusion | flops 1614807040 | bytes 9586688 | tf_op jit(solution)/shard_map/dot_general | solution.py:64
  926.0 9.4 fusion.4
  935.5 5.0 fusion.1
  940.5 12.5 %psum.140 = f32[512]{0:T(512)S(1)} all-reduce(f32[512]{0:T(512)S(1)} %get-tuple-element.5), channel_id=1, replica_groups=mesh['src'=32,'tgt'=8] {'tgt'}, use_global_device_ids=true, to_apply=%region_29.0 | all-reduce | flops 512 | bytes 4096 | tf_op jit(solution)/shard_map/psum | solution.py:65
  953.0 112.7 %psum.142 = f32[4096]{0:T(1024)S(1)} all-reduce(f32[4096]{0:T(1024)S(1)} %get-tuple-element.4), channel_id=1, replica_groups=mesh['src'=32,'tgt'=8] {'src'}, use_global_device_ids=true, to_apply=%region_32.0 | all-reduce | flops 4096 | bytes 32768 | tf_op jit(solution)/shard_map/psum | solution.py:69
  1067.3 66.1 %all-reduce.8.cloned.1.call-done = f32[64,4096]{1,0:T(8,128)} async-done(((f32[64,4096]{1,0:T(8,128)}), f32[64,4096]{1,0:T(8,128)}) %all-reduce.8.cloned.1.call-update) | async-done | bytes 1048592 | tf_op jit(solution)/shard_map/psum | solution.py:69
  (33 shorter events, 10.7 us)
Async XLA Ops:
  7.2 10.0 copy-start.3
  7.2 1058.5 %all-reduce.6.cloned.1.call-start = ((), (), s32[]{:S(2)}) async-start(), calls=%async_computation | async-start | bytes 262144 | tf_op jit(solution)/shard_map/psum | solution.py:65
  17.1 12.1 %copy-start = (f32[512,4096]{1,0:T(8,128)}, f32[512,4096]{1,0:T(8,128)S(1)}, u32[]{:S(2)}) copy-start(f32[512,4096]{1,0:T(8,128)S(1)} %get-tuple-element.30) | copy-start | bytes 25165828
  17.1 7.7 copy-start.5
  668.3 245.9 %copy-start.1 = (f32[64,4096]{1,0:T(8,128)S(1)}, f32[64,4096]{1,0:T(8,128)}, u32[]{:S(2)}) copy-start(f32[64,4096]{1,0:T(8,128)} %param.7) | copy-start | bytes 3145732
  787.7 138.3 %copy-start.2 = (f32[64,512]{1,0:T(8,128)S(1)}, f32[64,512]{1,0:T(8,128)}, u32[]{:S(2)}) copy-start(f32[64,512]{1,0:T(8,128)} %param.6) | copy-start | bytes 393220
  914.2 21.3 %copy-start.4 = (f32[4096]{0:T(1024)}, f32[4096]{0:T(1024)S(1)}, u32[]{:S(2)}) copy-start(f32[4096]{0:T(1024)S(1)} %multiply_add_fusion) | copy-start | bytes 49156
  926.0 207.4 %all-reduce.8.cloned.1.call-start = ((), (), s32[]{:S(2)}) async-start(), calls=%async_computation.1 | async-start | bytes 2097152 | tf_op jit(solution)/shard_map/psum | solution.py:69
Sparse Core Ops, SparseCore 0:
  926.1 56.6 all-reduce.5
  987.2 146.0 all-reduce.7
where the time goes:
time: 1160 us; the launch traced here: 1140 us
  blocking collectives  957 us (82%)
  matrix products  74.9 us (6%)
  waiting for transfers between devices  66.1 us (6%)
  between operations  28.9 us (2%)
  other arithmetic  15.6 us (1%)
    psum x5, blocking collectives, inner_product(): return lax.psum(local_term, ('src', 'tgt'))  395 us
    psum x3, blocking collectives, body(): col_out = lax.psum(jnp.dot(dir_src, plan_now, precision=HIGHEST), 'src')  342 us
    psum x1, blocking collectives, body(): col_weight, weighted_x = lax.psum((col_weight, weighted_x), 'src')  113 us
    psum x3, blocking collectives, body(): row_out = lax.psum(jnp.dot(plan_now, dir_tgt, precision=HIGHEST), 'tgt')  95.6 us
    psum x1, waiting for transfers between devices, body(): col_weight, weighted_x = lax.psum((col_weight, weighted_x), 'src')  66.1 us
    dot_general x3, matrix products, body(): row_out = lax.psum(jnp.dot(plan_now, dir_tgt, precision=HIGHEST), 'tgt')  26.5 us
  transfers between devices with their start and end apart: 2, of which 1 were waited for; matrix products, arithmetic and copies ran while one was open for 1% of the time, Pallas kernels for 0%

commit v1 on v0

v1 whole, which is shorter than its diff:
```python
import functools
import math

import jax
import jax.numpy as jnp
from jax import lax
from jax.experimental import pallas as pl
from jax.experimental.pallas import tpu as pltpu
from jax.sharding import PartitionSpec as P

EPSILON = 0.5
REGULARIZER = 1.0
LOG2E = math.log2(math.e)
MESH = pl.DeviceIdType.MESH
F32 = jnp.float32
BF16 = jnp.bfloat16

XS, ZS = 4, 8
SW, TW = XS * ZS, 8
DIM = 64
NS, NT = 512, 4096
SUB = NT // SW
TILE = 512
STACK = 80
VECS = 4

(A_COL, A_ROW, A_INIT, A_AGC, A_AGZ, A_AGS, B_COL, B_ROW, B_AGC, B_AGZ, B_AGS, C_SRC, C_TGT,
 D_ROW, D_COL, O_ROW, O_COL, G_NEAR, G_FAR, G_SIB1, G_SIB2) = range(21)
N_SEMS = 24
O_X = 20 + 4


def halves(value):
    high = value.astype(BF16)
    return high, (value - high.astype(F32)).astype(BF16)


def across(vector):
    return jnp.broadcast_to(vector, (128, vector.shape[1])).T


def along(block):
    return jnp.sum(block.T, axis=0, keepdims=True)


def tiled(block, times):
    return jnp.concatenate([block] * times, axis=1)


def total(value):
    return jnp.sum(jnp.sum(value, axis=1, keepdims=True), axis=0, keepdims=True)


def lanes(*values):
    spot = lax.broadcasted_iota(jnp.int32, (1, 128), 1)
    row = jnp.zeros((1, 128), F32)
    for index, value in enumerate(values):
        row = row + jnp.where(spot == index, value, 0.0)
    return row


def lane(row, index):
    spot = lax.broadcasted_iota(jnp.int32, (1, 128), 1)
    return jnp.sum(jnp.where(spot == index, row, 0.0), axis=1, keepdims=True)


def kernel(
    shift, xs_ref, yt_ref, f_ref, g_ref, a0_ref, b0_ref,
    sol_src_ref, sol_tgt_ref, gs_ref, gt_ref,
    plan, plan_hi, plan_lo, q_hi, q_lo, x4t, y4, zbuf, fcol, acol, racc, racc2,
    col_a, col_a_in, row_a, row_a_in, init_out, init_in, agc_a, agz_a, ags_a, ags_a_in,
    col_b, col_b_in, row_b, row_b_in, agc_b, agz_b, ags_b_in,
    sc_out, sc_in, sc2_out, sc2_in, ysub, vec_t, vec_s, stack, tsum,
    g_row, g_row_in, g_col, g_col_in, xg, send, recv,
):
    s = lax.axis_index("src")
    t = lax.axis_index("tgt")
    x, z = s // ZS, s % ZS
    core = t % 2
    sibling = (s, t + 1 - 2 * core)

    def src_peer(p):
        return (lax.rem(s + p, SW), t)

    def tgt_peer(p):
        return (s, lax.rem(t + p, TW))

    def z_peer(p):
        return (x * ZS + lax.rem(z + p, ZS), t)

    def x_peer(p):
        return (lax.rem(x + p, XS) * ZS + z, t)

    def push(src, dst, k, device, k_recv=None):
        pltpu.make_async_remote_copy(
            src_ref=src, dst_ref=dst, send_sem=send.at[k],
            recv_sem=recv.at[k if k_recv is None else k_recv],
            device_id=device, device_id_type=MESH,
        ).start()

    def push_all(ways, peer, src, dst, k):
        def step(p, carry):
            push(src(p), dst, k, peer(p))
            return carry
        lax.fori_loop(1, ways, step, 0)

    def wait_in(ref, k):
        pltpu.make_async_copy(ref, ref, recv.at[k]).wait()

    def wait_out(ref, k):
        pltpu.make_async_copy(ref, ref, send.at[k]).wait()

    def sub_of(p):
        return pl.ds(pl.multiple_of(lax.rem(s + p, SW) * SUB, SUB), SUB)

    my_sub = pl.ds(pl.multiple_of(s * SUB, SUB), SUB)
    my_tile = pl.ds(pl.multiple_of(z * TILE, TILE), TILE)

    barrier = pltpu.get_barrier_semaphore()

    def greet(ways, peer):
        def step(p, carry):
            pl.semaphore_signal(barrier, inc=1, device_id=peer(p), device_id_type=MESH)
            return carry
        lax.fori_loop(1, ways, step, 0)

    greet(SW, src_peer)
    greet(TW, tgt_peer)

    xs = jnp.concatenate([xs_ref[0], xs_ref[1]], axis=0)
    a0 = a0_ref[...]
    b0 = b0_ref[...]

    def x_parts(points):
        scaled = points * (LOG2E / EPSILON)
        high = scaled.astype(BF16).astype(F32)
        low = scaled - high
        return jnp.concatenate([high, high, low, low], axis=0).T.astype(BF16)

    x4t[...] = x_parts(xs)

    def y_step(n, carry):
        cs = pl.ds(pl.multiple_of(n * TILE, TILE), TILE)
        high, low = halves(yt_ref[:, cs])
        y4[0:64, cs] = high
        y4[64:128, cs] = low
        y4[128:192, cs] = high
        y4[192:256, cs] = low
        return carry
    lax.fori_loop(0, NT // TILE, y_step, 0)

    fcol[...] = across(f_ref[...] * LOG2E + shift)
    acol[...] = across(a0)
    racc[...] = jnp.zeros_like(racc)
    racc2[...] = jnp.zeros_like(racc2)

    def plan_step(n, carry):
        cs = pl.ds(pl.multiple_of(n * TILE, TILE), TILE)
        zbuf[...] = jnp.dot(x4t[...], y4[:, cs], preferred_element_type=F32)
        g_now = g_ref[:, cs] * LOG2E
        b_now = b0_ref[:, cs]

        def rows_step(r, sums):
            rows = pl.ds(pl.multiple_of(r * 64, 64), 64)
            p = jnp.exp2(zbuf[rows, :] + tiled(fcol[rows, :], 4) + g_now)
            plan[rows, cs] = p
            high, low = halves(p)
            plan_hi[rows, cs] = high
            plan_lo[rows, cs] = low
            racc[rows, :] += (p[:, 0:128] + p[:, 128:256]) + (p[:, 256:384] + p[:, 384:512])
            pb = p * b_now
            racc2[rows, :] += (pb[:, 0:128] + pb[:, 128:256]) + (pb[:, 256:384] + pb[:, 384:512])
            pa = p * tiled(acol[rows, :], 4)
            return (sums[0] + jnp.sum(p.reshape(8, 8, TILE), axis=0),
                    sums[1] + jnp.sum(pa.reshape(8, 8, TILE), axis=0))

        zero = jnp.zeros((8, TILE), F32)
        mass_sum, a_sum = lax.fori_loop(0, NS // 64, rows_step, (zero, zero))
        col_a[0:1, cs] = jnp.sum(mass_sum, axis=0, keepdims=True)
        col_a[1:2, cs] = jnp.sum(a_sum, axis=0, keepdims=True)
        return carry
    lax.fori_loop(0, NT // TILE, plan_step, 0)

    mass_part = along(racc[...])
    v_part = along(racc2[...])
    row_a[0:1, :] = mass_part
    row_a[1:2, :] = v_part
    init_out[0:1, :] = f_ref[...]
    init_out[1:2, :] = a0
    norm_part = total(a0 * a0) * (1.0 / TW) + total(b0 * b0) * (1.0 / SW)
    quad_part = (
        norm_part * REGULARIZER
        + total(a0 * a0 * mass_part) + total(b0 * b0 * col_a[0:1, :]) + 2.0 * total(a0 * v_part)
    )
    col_a[2:3, :] = tiled(lanes(norm_part, quad_part), SW)
    col_a[3:4, :] = jnp.zeros((1, NT), F32)

    pl.semaphore_wait(barrier, SW - 1 + TW - 1)

    push_all(SW, src_peer, lambda p: col_a.at[:, sub_of(p)], col_a_in.at[s], A_COL)
    push_all(TW, tgt_peer, lambda p: row_a, row_a_in.at[t], A_ROW)
    push_all(ZS, z_peer, lambda p: init_out, init_in.at[z], A_INIT)
    for p in (1, ZS - 1, 2, ZS - 2):
        push(xs_ref.at[core], xg.at[z, core], G_NEAR, z_peer(p))
    col_a_in[s] = col_a[:, my_sub]
    row_a_in[t] = row_a[...]
    init_in[z] = init_out[...]
    xg[z, 0] = xs_ref[0]
    xg[z, 1] = xs_ref[1]
    ysub[...] = yt_ref[:, my_tile]

    g_sub = g_ref[:, my_tile] * LOG2E

    def q_block(p, carry):
        zz = lax.rem(z + p, ZS)
        points = jnp.concatenate([xg[zz, 0], xg[zz, 1]], axis=0)
        fcol[...] = across(init_in[zz][0:1, :] * LOG2E + shift)
        zbuf[...] = jnp.dot(x_parts(points), y4[:, my_tile], preferred_element_type=F32)

        def rows_step(r, c):
            rows = pl.ds(pl.multiple_of(r * 64, 64), 64)
            value = jnp.exp2(zbuf[rows, :] + tiled(fcol[rows, :], 4) + g_sub)
            high, low = halves(value)
            q_hi[zz, rows, :] = high
            q_lo[zz, rows, :] = low
            return c
        lax.fori_loop(0, NS // 64, rows_step, 0)
        return carry

    wait_in(row_a_in.at[pl.ds(0, TW - 1)], A_ROW)
    row_full = jnp.sum(row_a_in[...], axis=0)
    agz_own = row_full
    wait_in(col_a_in.at[pl.ds(0, SW - 1)], A_COL)
    col_full = jnp.sum(col_a_in[...], axis=0)
    agc_a[:, my_sub] = col_full[0:2, :]
    ags_a[...] = col_full[2:3, :]
    agz_a[z] = agz_own

    push_all(SW, src_peer, lambda p: agc_a.at[:, my_sub], agc_a.at[:, my_sub], A_AGC)
    push_all(TW, tgt_peer, lambda p: ags_a, ags_a_in.at[t], A_AGS)
    push_all(ZS, z_peer, lambda p: agz_a.at[z], agz_a.at[z], A_AGZ)
    ags_a_in[t] = ags_a[...]
    wait_in(init_in.at[pl.ds(0, ZS - 1)], A_INIT)
    wait_in(xg.at[pl.ds(0, 4), 0], G_NEAR)
    for p in (1, ZS - 1, 2, ZS - 2):
        zz = lax.rem(z + p, ZS)
        push(xg.at[zz, core], xg.at[zz, core], G_SIB1, sibling)
    for p in (3, ZS - 3, 4):
        push(xs_ref.at[core], xg.at[z, core], G_FAR, z_peer(p))
    q_block(0, 0)

    wait_in(agz_a.at[pl.ds(0, ZS - 1)], A_AGZ)
    wait_in(ags_a_in.at[pl.ds(0, TW - 1)], A_AGS)
    wait_in(agc_a.at[:, pl.ds(0, (SW - 1) * SUB)], A_AGC)
    sums = jnp.sum(ags_a_in[...], axis=0)
    norm0 = lane(sums, 0)
    alpha0 = norm0 / lane(sums, 1)

    diag = [row_full[0:1, :] + REGULARIZER, agz_a[:, 0, :] + REGULARIZER, agc_a[0:1, :] + REGULARIZER]
    res0 = [a0, init_in[:, 1, :], b0]
    prod0 = [row_full[1:2, :], agz_a[:, 1, :], agc_a[1:2, :]]
    image0 = [d * r + v for d, r, v in zip(diag, res0, prod0)]
    res1 = [r - alpha0 * i for r, i in zip(res0, image0)]

    def matvec(vec_src, vec_tgt, columns):
        acol[...] = across(vec_src)
        half = NT // 2
        for h, acc in ((0, racc), (1, racc2)):
            spread = jnp.broadcast_to(vec_tgt[:, h * half:(h + 1) * half], (8, half))

            def step(r, sums):
                rows = pl.ds(pl.multiple_of(r * 8, 8), 8)
                p = plan[rows, h * half:(h + 1) * half]
                terms = p * spread
                parts = [terms[:, k * 128:(k + 1) * 128] for k in range(half // 128)]
                while len(parts) > 1:
                    parts = [parts[k] + parts[k + 1] for k in range(0, len(parts), 2)]
                acc[rows, :] = parts[0]
                if columns:
                    sums = sums + p * tiled(acol[rows, :], half // 128)
                return sums
            sums = lax.fori_loop(0, NS // 8, step, jnp.zeros((8, half), F32), unroll=2)
            if columns:
                col_b[0:1, h * half:(h + 1) * half] = jnp.sum(sums, axis=0, keepdims=True)
        return along(racc[...] + racc2[...])

    def scalars(res, row_part):
        norm = total(res[0] * res[0]) * (1.0 / TW) + total(res[2] * res[2]) * (1.0 / SW)
        quad = (
            total(res[0] * res[0] * diag[0]) * (1.0 / TW)
            + total(res[2] * res[2] * diag[2]) * (1.0 / SW)
            + 2.0 * total(res[0] * row_part)
        )
        return lanes(norm, quad)

    row_part = matvec(res1[0], res1[2], True)
    row_b[...] = row_part
    col_b[1:2, :] = tiled(scalars(res1, row_part), SW)

    push_all(SW, src_peer, lambda p: col_b.at[:, sub_of(p)], col_b_in.at[s], B_COL)
    push_all(TW, tgt_peer, lambda p: row_b, row_b_in.at[t], B_ROW)
    col_b_in[s] = col_b[:, my_sub]
    row_b_in[t] = row_b[...]
    wait_in(xg.at[pl.ds(0, 3), 0], G_FAR)
    for p in (3, ZS - 3, 4):
        zz = lax.rem(z + p, ZS)
        push(xg.at[zz, core], xg.at[zz, core], G_SIB2, sibling)
    wait_in(xg.at[pl.ds(0, 4), 0], G_SIB1)
    lax.fori_loop(1, 3, q_block, 0)
    lax.fori_loop(6, 8, q_block, 0)

    wait_in(row_b_in.at[pl.ds(0, TW - 1)], B_ROW)
    row_full1 = jnp.sum(row_b_in[...], axis=0)
    agz_b[z] = row_full1
    wait_in(col_b_in.at[pl.ds(0, SW - 1)], B_COL)
    col_full1 = jnp.sum(col_b_in[...], axis=0)
    agc_b[:, my_sub] = col_full1[0:1, :]
    sc2_out[0] = col_full1[1:2, :]

    push_all(SW, src_peer, lambda p: agc_b.at[:, my_sub], agc_b.at[:, my_sub], B_AGC)
    push_all(TW, tgt_peer, lambda p: sc2_out.at[0], ags_b_in.at[t], B_AGS)
    push_all(ZS, z_peer, lambda p: agz_b.at[z], agz_b.at[z], B_AGZ)
    ags_b_in[t] = sc2_out[0]
    wait_in(xg.at[pl.ds(0, 3), 0], G_SIB2)
    lax.fori_loop(3, 6, q_block, 0)

    wait_in(agz_b.at[pl.ds(0, ZS - 1)], B_AGZ)
    wait_in(ags_b_in.at[pl.ds(0, TW - 1)], B_AGS)
    wait_in(agc_b.at[:, pl.ds(0, (SW - 1) * SUB)], B_AGC)
    sums = jnp.sum(ags_b_in[...], axis=0)
    norm1 = lane(sums, 0)
    beta0 = norm1 / norm0
    alpha1 = norm1 / (lane(sums, 1) - beta0 * norm1 / alpha0)
    prod1 = [row_full1, agz_b[:, 0, :], agc_b[...]]
    dir1 = [r1 + beta0 * r0 for r1, r0 in zip(res1, res0)]
    image1 = [d * r + v + beta0 * i for d, r, v, i in zip(diag, res1, prod1, image0)]
    res2 = [r - alpha1 * i for r, i in zip(res1, image1)]
    sol2 = [alpha0 * r0 + alpha1 * d1 for r0, d1 in zip(res0, dir1)]

    row_part = matvec(res2[0], res2[2], False)
    sc_out[...] = scalars(res2, row_part)

    push_all(SW, src_peer, lambda p: sc_out, sc_in.at[s], C_SRC)
    sc_in[s] = sc_out[...]

    vec_t[0:1, :] = jnp.ones((1, NT), F32)
    vec_t[1:2, :] = sol2[2]
    vec_t[2:3, :] = dir1[2]
    vec_t[3:4, :] = res2[2]
    vec_s[:, 0, :] = jnp.ones((ZS, NS), F32)
    vec_s[:, 1, :] = sol2[1]
    vec_s[:, 2, :] = dir1[1]
    vec_s[:, 3, :] = res2[1]

    def fill_stack(points, weights):
        for v in range(VECS):
            weight = weights[v:v + 1, :]
            value = jnp.concatenate([points * weight, jnp.broadcast_to(weight, (16, TILE))], axis=0)
            high, low = halves(value)
            stack[v * STACK:(v + 1) * STACK, :] = high
            stack[(VECS + v) * STACK:(VECS + v + 1) * STACK, :] = low

    def gather_sums(high, low, dims):
        first = lax.dot_general(stack[...], high, (dims, ((), ())), preferred_element_type=F32)
        second = lax.dot_general(
            stack[0:VECS * STACK, :], low, (dims, ((), ())), preferred_element_type=F32
        )
        tsum[...] += first[0:VECS * STACK, :] + first[VECS * STACK:, :] + second

    def gradients(points, own, write):
        ones = tsum[0:64, :], tsum[64:65, :]
        base = points * ones[1] - ones[0]
        for v in range(1, VECS):
            low = v * STACK
            part = points * tsum[low + 64:low + 65, :] - tsum[low:low + 64, :]
            weight = own[v] + 1.0 if v == 1 else own[v]
            write(v - 1, base * weight + part)

    tsum[...] = jnp.zeros_like(tsum)

    def col_step(zz, carry):
        fill_stack(jnp.concatenate([xg[zz, 0], xg[zz, 1]], axis=0), vec_s[zz])
        gather_sums(q_hi[zz], q_lo[zz], ((1,), (0,)))
        return carry
    lax.fori_loop(0, ZS, col_step, 0)

    def write_col(part, value):
        for k in range(XS):
            g_col[part, k] = value[k * 16:(k + 1) * 16, :]
    own_t = vec_t[:, my_tile]
    gradients(ysub[...], [own_t[v:v + 1, :] for v in range(VECS)], write_col)
    push_all(XS, x_peer, lambda p: g_col.at[:, lax.rem(x + p, XS)], g_col_in.at[x], D_COL)
    g_col_in[x] = g_col[:, x]

    wait_in(sc_in.at[pl.ds(0, SW - 1)], C_SRC)
    sc2_out[1] = jnp.sum(sc_in[...], axis=0)
    push_all(TW, tgt_peer, lambda p: sc2_out.at[1], sc2_in.at[t], C_TGT)
    sc2_in[t] = sc2_out[1]

    tsum[...] = jnp.zeros_like(tsum)

    def row_step(n, carry):
        cs = pl.ds(pl.multiple_of(n * TILE, TILE), TILE)
        fill_stack(yt_ref[:, cs], vec_t[:, cs])
        gather_sums(plan_hi[:, cs], plan_lo[:, cs], ((1,), (1,)))
        return carry
    lax.fori_loop(0, NT // TILE, row_step, 0)

    def write_row(part, value):
        for k in range(TW):
            g_row[part, k] = value[k * 8:(k + 1) * 8, :]
    gradients(xs, [None, sol2[0], dir1[0], res2[0]], write_row)
    push_all(TW, tgt_peer, lambda p: g_row.at[:, lax.rem(t + p, TW)], g_row_in.at[t], D_ROW)
    g_row_in[t] = g_row[:, t]

    wait_in(sc2_in.at[pl.ds(0, TW - 1)], C_TGT)
    sums = jnp.sum(sc2_in[...], axis=0)
    norm2 = lane(sums, 0)
    beta1 = norm2 / norm1
    alpha2 = norm2 / (lane(sums, 1) - beta1 * norm2 / alpha1)
    both = alpha2 * beta1

    def combine(parts):
        return (parts[0] + both * parts[1] + alpha2 * parts[2]) * (1.0 / EPSILON)

    wait_in(g_col_in.at[pl.ds(0, XS - 1)], D_COL)
    gt_ref[x, :, my_tile] = combine(jnp.sum(g_col_in[...], axis=0))
    for dx in range(XS):
        def step(p, carry):
            device = (lax.rem(x + dx, XS) * ZS + lax.rem(z + p, ZS), t)
            push(gt_ref.at[x, :, my_tile], gt_ref.at[x, :, my_tile], O_COL, device, O_X + dx)
            return carry
        lax.fori_loop(1 if dx == 0 else 0, ZS, step, 0)

    wait_in(g_row_in.at[pl.ds(0, TW - 1)], D_ROW)
    gs_ref[t] = combine(jnp.sum(g_row_in[...], axis=0))
    push_all(TW, tgt_peer, lambda p: gs_ref.at[t], gs_ref.at[t], O_ROW)

    sol_src_ref[...] = sol2[0] + both * dir1[0] + alpha2 * res2[0]
    sol_tgt_ref[...] = sol2[2] + both * dir1[2] + alpha2 * res2[2]

    wait_in(gs_ref.at[pl.ds(0, TW - 1)], O_ROW)
    wait_in(gt_ref.at[x, :, pl.ds(0, (ZS - 1) * TILE)], O_X)
    for dx in range(1, XS):
        wait_in(gt_ref.at[lax.rem(x + XS - dx, XS)], O_X + dx)

    wait_out(col_a_in.at[pl.ds(0, SW - 1)], A_COL)
    wait_out(row_a_in.at[pl.ds(0, TW - 1)], A_ROW)
    wait_out(init_in.at[pl.ds(0, ZS - 1)], A_INIT)
    wait_out(agc_a.at[:, pl.ds(0, (SW - 1) * SUB)], A_AGC)
    wait_out(agz_a.at[pl.ds(0, ZS - 1)], A_AGZ)
    wait_out(ags_a_in.at[pl.ds(0, TW - 1)], A_AGS)
    wait_out(col_b_in.at[pl.ds(0, SW - 1)], B_COL)
    wait_out(row_b_in.at[pl.ds(0, TW - 1)], B_ROW)
    wait_out(agc_b.at[:, pl.ds(0, (SW - 1) * SUB)], B_AGC)
    wait_out(agz_b.at[pl.ds(0, ZS - 1)], B_AGZ)
    wait_out(ags_b_in.at[pl.ds(0, TW - 1)], B_AGS)
    wait_out(sc_in.at[pl.ds(0, SW - 1)], C_SRC)
    wait_out(sc2_in.at[pl.ds(0, TW - 1)], C_TGT)
    wait_out(g_row_in.at[pl.ds(0, TW - 1)], D_ROW)
    wait_out(g_col_in.at[pl.ds(0, XS - 1)], D_COL)
    wait_out(gs_ref.at[pl.ds(0, TW - 1)], O_ROW)
    wait_out(gt_ref.at[pl.ds(0, 3)], O_COL)
    wait_out(gt_ref.at[0, :, pl.ds(0, (ZS - 1) * TILE)], O_COL)
    wait_out(xg.at[pl.ds(0, 4), 0], G_NEAR)
    wait_out(xg.at[pl.ds(0, 3), 0], G_FAR)
    wait_out(xg.at[pl.ds(0, 4), 0], G_SIB1)
    wait_out(xg.at[pl.ds(0, 3), 0], G_SIB2)


def body(src_points, tgt_points, src_potential, tgt_potential, src_rhs, tgt_rhs):
    normalizer = 1.0 / math.sqrt(NS * SW * NT * TW)
    vmem = pl.BlockSpec(memory_space=pltpu.VMEM)

    def buf(*shape, dtype=F32):
        return pltpu.VMEM(shape, dtype)

    scratch = [
        buf(NS, NT), buf(NS, NT, dtype=BF16), buf(NS, NT, dtype=BF16),
        buf(ZS, NS, TILE, dtype=BF16), buf(ZS, NS, TILE, dtype=BF16),
        buf(NS, 256, dtype=BF16), buf(256, NT, dtype=BF16), buf(NS, TILE),
        buf(NS, 128), buf(NS, 128), buf(NS, 128), buf(NS, 128),
        buf(4, NT), buf(SW, 4, SUB), buf(2, NS), buf(TW, 2, NS),
        buf(2, NS), buf(ZS, 2, NS),
        buf(2, NT), buf(ZS, 2, NS), buf(1, 128), buf(TW, 1, 128),
        buf(2, NT), buf(SW, 2, SUB), buf(1, NS), buf(TW, 1, NS),
        buf(1, NT), buf(ZS, 1, NS), buf(TW, 1, 128),
        buf(1, 128), buf(SW, 1, 128), buf(2, 1, 128), buf(TW, 1, 128),
        buf(DIM, TILE), buf(VECS, NT), buf(ZS, VECS, NS),
        buf(2 * VECS * STACK, TILE, dtype=BF16), buf(VECS * STACK, TILE),
        buf(3, TW, 8, NS), buf(TW, 3, 8, NS),
        buf(3, XS, 16, TILE), buf(XS, 3, 16, TILE),
        buf(ZS, 2, DIM // 2, NS),
        pltpu.SemaphoreType.DMA((N_SEMS,)), pltpu.SemaphoreType.DMA((O_X + XS,)),
    ]
    sol_src, sol_tgt, grad_src, grad_tgt = pl.pallas_call(
        functools.partial(kernel, math.log2(normalizer)),
        out_shape=(
            jax.ShapeDtypeStruct((1, NS), F32),
            jax.ShapeDtypeStruct((1, NT), F32),
            jax.ShapeDtypeStruct((TW, 8, NS), F32),
            jax.ShapeDtypeStruct((XS, 16, NT), F32),
        ),
        in_specs=[vmem] * 6,
        out_specs=[vmem] * 4,
        scratch_shapes=scratch,
        compiler_params=pltpu.CompilerParams(
            collective_id=1, has_side_effects=True, vmem_limit_bytes=56 * 1024 * 1024
        ),
    )(
        src_points.reshape(2, DIM // 2, NS), tgt_points, src_potential.reshape(1, NS),
        tgt_potential.reshape(1, NT), src_rhs.reshape(1, NS), tgt_rhs.reshape(1, NT),
    )
    return (
        sol_src.reshape(NS), sol_tgt.reshape(NT), grad_src.reshape(DIM, NS), grad_tgt.reshape(DIM, NT)
    )


def solution(mesh):
    return jax.shard_map(
        body,
        mesh=mesh,
        in_specs=(P(None, "src"), P(None, "tgt"), P("src"), P("tgt"), P("src"), P("tgt")),
        out_specs=(P("src"), P("tgt"), P(None, "src"), P(None, "tgt")),
        check_vma=False,
    )
```

time: 1160 us -> 89.1 us (0.08); the launches traced: 1140 us -> 87.9 us
  blocking collectives: 957 us -> 0 us
  Pallas kernels: 0 us -> 81.6 us
  matrix products: 74.9 us -> 0 us
  waiting for transfers between devices: 66.1 us -> 0 us
  between operations: 28.9 us -> 0.65 us
  other arithmetic: 15.6 us -> 0 us
    psum x13 -> x0, blocking collectives: 957 us -> none  [the longest x5 395 us: inner_product(): return lax.psum(local_term, ('src', 'tgt'))]
    pallas_call x0 -> x1, Pallas kernels: none -> 81.6 us  [body(): pl.pallas_call(functools.partial(kernel, math.log2(normalizer)), out_shap...]
    dot_general x9 -> x0, matrix products: 74.9 us -> none  [the longest x3 26.5 us: body(): row_out = lax.psum(jnp.dot(plan_now, dir_tgt, precision=HIGHEST), 'tgt')]
    psum x2 -> x0, waiting for transfers between devices: 66.1 us -> none  [the longest x1 66.1 us: body(): col_weight, weighted_x = lax.psum((col_weight, weighted_x), 'src')]
  transfers between devices with their start and end apart: 2 -> 0, of which waited for: 1 -> 0; matrix products, arithmetic and copies ran while one was open for 1% -> 0% of each run, Pallas kernels for 0% -> 0%
where the time goes in v1:
time: 89.1 us; the launch traced here: 87.9 us
  Pallas kernels  81.6 us (92%)
  local copies, waits for them, and re-layouts  5.71 us (6%)
    pallas_call x1, Pallas kernels, body(): pl.pallas_call(functools.partial(kernel, math.log2(normalizer)), out_shap...  81.6 us
    unnamed x6, local copies, waits for them, and re-layouts  5.71 us

profile of v1, /device:TPU:1, one launch (start us, length us, event | category | flops | bytes accessed | tf_op | source)
XLA Modules:
  0.0 87.9 jit_solution(7356576779104487499)
XLA Ops:
  0.6 81.6 %shard_map.93 = (f32[1,512]{1,0:T(1,128)}, f32[1,4096]{1,0:T(1,128)}, f32[8,8,512]{2,1,0:T(8,128)}, f32[4,16,4096]{2,1,0:T(8,128)}) custom-call(f32[2,32,512]{2,1,0:T(8,128)} %bitcast.10, f32[64,4096]{1,0:T(8,128)} %yt_ref.1, f32[1,512]{1,0:T(1,128)} %bitcast.15, f32[1,4096]{1,0:T(1,128)} %bitcast.12, f32[1,512]{1,0:T(1,128)} %bitcast.16, f32[1,4096]{1,0:T(1,128)} %bitcast.13), custom_call_target="tpu_custom_call" | custom-call | tf_op jit(solution)/shard_map/pallas_call | solution.py:496
  82.2 0.0 copy-start
  82.2 1.3 %copy.14 = f32[512]{0:T(512)} copy(f32[512]{0:T(512)} %bitcast.17) | data formatting | bytes 4096
  83.5 0.0 copy-done
  83.5 0.6 copy.15
  84.1 1.6 %copy.16 = f32[64,512]{1,0:T(8,128)} copy(f32[64,512]{1,0:T(8,128)} %bitcast.11) | data formatting | bytes 262144
  85.7 2.3 %copy.17 = f32[64,4096]{1,0:T(8,128)} copy(f32[64,4096]{1,0:T(8,128)} %bitcast.9) | data formatting | bytes 2097152
Async XLA Ops:
  82.2 1.3 %copy-start = (f32[1,4096]{1,0:T(1,128)S(1)}, f32[1,4096]{1,0:T(1,128)}, u32[]{:S(2)}) copy-start(f32[1,4096]{1,0:T(1,128)} %get-tuple-element.9) | copy-start | bytes 49156

commit v2 on v1

--- a/solution.py
+++ b/solution.py
@@ -25,9 +25,12 @@
 VECS = 4
 
 (A_COL, A_ROW, A_INIT, A_AGC, A_AGZ, A_AGS, B_COL, B_ROW, B_AGC, B_AGZ, B_AGS, C_SRC, C_TGT,
- D_ROW, D_COL, O_ROW, O_COL, G_NEAR, G_FAR, G_SIB1, G_SIB2) = range(21)
-N_SEMS = 24
-O_X = 20 + 4
+ D_ROW, D_COL, D_ROW2, D_COL2, O_ROW, O_XX, O_XZ, O_ZF, G_NEAR, G_FAR, G_SIB1, G_SIB2) = range(25)
+IN_ZF = 25
+IN_XF = IN_ZF + ZS
+N_SEMS = 25
+N_IN = IN_XF + XS
+LEAD = 384
 
 
 def halves(value):
@@ -65,14 +68,23 @@
 
 
 def kernel(
-    shift, xs_ref, yt_ref, f_ref, g_ref, a0_ref, b0_ref,
+    shift, xs_hbm, yt_hbm, f_hbm, g_hbm, a0_hbm, b0_hbm,
     sol_src_ref, sol_tgt_ref, gs_ref, gt_ref,
-    plan, plan_hi, plan_lo, q_hi, q_lo, x4t, y4, zbuf, fcol, acol, racc, racc2,
+    xs_ref, yt_ref, f_ref, g_ref, a0_ref, b0_ref, load,
+    plan, plan_hi, plan_lo, q_hi, q_lo, x4t, y4, fcol, acol, racc, racc2,
     col_a, col_a_in, row_a, row_a_in, init_out, init_in, agc_a, agz_a, ags_a, ags_a_in,
     col_b, col_b_in, row_b, row_b_in, agc_b, agz_b, ags_b_in,
-    sc_out, sc_in, sc2_out, sc2_in, ysub, vec_t, vec_s, stack, tsum,
+    sc_out, sc_in, sc2_out, sc2_in, ysub, vec_t, vec_s, stack, t_row, t_col,
     g_row, g_row_in, g_col, g_col_in, xg, send, recv,
 ):
+    loads = [
+        pltpu.make_async_copy(far, near, load.at[k])
+        for k, (far, near) in enumerate((
+            (yt_hbm, yt_ref), (xs_hbm, xs_ref), (f_hbm, f_ref), (g_hbm, g_ref), (a0_hbm, a0_ref), (b0_hbm, b0_ref),
+        ))
+    ]
+    for copy in loads:
+        copy.start()
     s = lax.axis_index("src")
     t = lax.axis_index("tgt")
     x, z = s // ZS, s % ZS
@@ -126,6 +138,8 @@
 
     greet(SW, src_peer)
     greet(TW, tgt_peer)
+    for copy in loads:
+        copy.wait()
 
     xs = jnp.concatenate([xs_ref[0], xs_ref[1]], axis=0)
     a0 = a0_ref[...]
@@ -156,26 +170,20 @@
 
     def plan_step(n, carry):
         cs = pl.ds(pl.multiple_of(n * TILE, TILE), TILE)
-        zbuf[...] = jnp.dot(x4t[...], y4[:, cs], preferred_element_type=F32)
+        cross = jnp.dot(x4t[...], y4[:, cs], preferred_element_type=F32)
         g_now = g_ref[:, cs] * LOG2E
         b_now = b0_ref[:, cs]
-
-        def rows_step(r, sums):
-            rows = pl.ds(pl.multiple_of(r * 64, 64), 64)
-            p = jnp.exp2(zbuf[rows, :] + tiled(fcol[rows, :], 4) + g_now)
-            plan[rows, cs] = p
-            high, low = halves(p)
-            plan_hi[rows, cs] = high
-            plan_lo[rows, cs] = low
-            racc[rows, :] += (p[:, 0:128] + p[:, 128:256]) + (p[:, 256:384] + p[:, 384:512])
+        mass_sum = jnp.zeros((8, TILE), F32)
+        a_sum = jnp.zeros((8, TILE), F32)
+        for r in range(0, NS, 64):
+            p = jnp.exp2(cross[r:r + 64, :] + tiled(fcol[r:r + 64, :], 4) + g_now)
+            plan[r:r + 64, cs] = p
+            racc[r:r + 64, :] += (p[:, 0:128] + p[:, 128:256]) + (p[:, 256:384] + p[:, 384:512])
             pb = p * b_now
-            racc2[rows, :] += (pb[:, 0:128] + pb[:, 128:256]) + (pb[:, 256:384] + pb[:, 384:512])
-            pa = p * tiled(acol[rows, :], 4)
-            return (sums[0] + jnp.sum(p.reshape(8, 8, TILE), axis=0),
-                    sums[1] + jnp.sum(pa.reshape(8, 8, TILE), axis=0))
-
-        zero = jnp.zeros((8, TILE), F32)
-        mass_sum, a_sum = lax.fori_loop(0, NS // 64, rows_step, (zero, zero))
+            racc2[r:r + 64, :] += (pb[:, 0:128] + pb[:, 128:256]) + (pb[:, 256:384] + pb[:, 384:512])
+            pa = p * tiled(acol[r:r + 64, :], 4)
+            mass_sum = mass_sum + jnp.sum(p.reshape(8, 8, TILE), axis=0)
+            a_sum = a_sum + jnp.sum(pa.reshape(8, 8, TILE), axis=0)
         col_a[0:1, cs] = jnp.sum(mass_sum, axis=0, keepdims=True)
         col_a[1:2, cs] = jnp.sum(a_sum, axis=0, keepdims=True)
         return carry
@@ -215,17 +223,61 @@
         zz = lax.rem(z + p, ZS)
         points = jnp.concatenate([xg[zz, 0], xg[zz, 1]], axis=0)
         fcol[...] = across(init_in[zz][0:1, :] * LOG2E + shift)
-        zbuf[...] = jnp.dot(x_parts(points), y4[:, my_tile], preferred_element_type=F32)
-
-        def rows_step(r, c):
-            rows = pl.ds(pl.multiple_of(r * 64, 64), 64)
-            value = jnp.exp2(zbuf[rows, :] + tiled(fcol[rows, :], 4) + g_sub)
+        cross = jnp.dot(x_parts(points), y4[:, my_tile], preferred_element_type=F32)
+        for r in range(0, NS, 64):
+            value = jnp.exp2(cross[r:r + 64, :] + tiled(fcol[r:r + 64, :], 4) + g_sub)
             high, low = halves(value)
-            q_hi[zz, rows, :] = high
-            q_lo[zz, rows, :] = low
-            return c
-        lax.fori_loop(0, NS // 64, rows_step, 0)
+            q_hi[zz, r:r + 64, :] = high
+            q_lo[zz, r:r + 64, :] = low
         return carry
+
+    def fill_stack(points, weights):
+        count = len(weights)
+        for v, weight in enumerate(weights):
+            value = jnp.concatenate([points * weight, jnp.broadcast_to(weight, (16, TILE))], axis=0)
+            high, low = halves(value)
+            stack[v * STACK:(v + 1) * STACK, :] = high
+            stack[(count + v) * STACK:(count + v + 1) * STACK, :] = low
+
+    def add_sums(out, low, count, plan_high, plan_low, dims):
+        rows = count * STACK
+        first = lax.dot_general(
+            stack[0:2 * rows, :], plan_high, (dims, ((), ())), preferred_element_type=F32
+        )
+        second = lax.dot_general(
+            stack[0:rows, :], plan_low, (dims, ((), ())), preferred_element_type=F32
+        )
+        out[low * STACK:low * STACK + rows, :] += first[0:rows, :] + first[rows:, :] + second
+
+    def row_sums(low, high, split=False):
+        def step(n, carry):
+            cs = pl.ds(pl.multiple_of(n * TILE, TILE), TILE)
+            if split:
+                for r in range(0, NS, 64):
+                    top, rest = halves(plan[r:r + 64, cs])
+                    plan_hi[r:r + 64, cs] = top
+                    plan_lo[r:r + 64, cs] = rest
+            fill_stack(yt_ref[:, cs], [vec_t[v:v + 1, cs] for v in range(low, high)])
+            add_sums(t_row, low, high - low, plan_hi[:, cs], plan_lo[:, cs], ((1,), (1,)))
+            return carry
+        lax.fori_loop(0, NT // TILE, step, 0)
+
+    def col_sums(low, high):
+        def step(zz, carry):
+            fill_stack(
+                jnp.concatenate([xg[zz, 0], xg[zz, 1]], axis=0),
+                [vec_s[zz, v:v + 1, :] for v in range(low, high)],
+            )
+            add_sums(t_col, low, high - low, q_hi[zz], q_lo[zz], ((1,), (0,)))
+            return carry
+        lax.fori_loop(0, ZS, step, 0)
+
+    t_row[...] = jnp.zeros_like(t_row)
+    t_col[...] = jnp.zeros_like(t_col)
+    vec_t[0:1, :] = jnp.ones((1, NT), F32)
+    vec_t[1:2, :] = b0
+    vec_s[:, 0, :] = jnp.ones((ZS, NS), F32)
+    row_sums(0, 2, split=True)
 
     wait_in(row_a_in.at[pl.ds(0, TW - 1)], A_ROW)
     row_full = jnp.sum(row_a_in[...], axis=0)
@@ -248,6 +300,9 @@
     for p in (3, ZS - 3, 4):
         push(xs_ref.at[core], xg.at[z, core], G_FAR, z_peer(p))
     q_block(0, 0)
+    wait_in(xg.at[pl.ds(0, 4), 0], G_SIB1)
+    lax.fori_loop(1, 3, q_block, 0)
+    lax.fori_loop(6, 8, q_block, 0)
 
     wait_in(agz_a.at[pl.ds(0, ZS - 1)], A_AGZ)
     wait_in(ags_a_in.at[pl.ds(0, TW - 1)], A_AGS)
@@ -305,9 +360,12 @@
     for p in (3, ZS - 3, 4):
         zz = lax.rem(z + p, ZS)
         push(xg.at[zz, core], xg.at[zz, core], G_SIB2, sibling)
-    wait_in(xg.at[pl.ds(0, 4), 0], G_SIB1)
-    lax.fori_loop(1, 3, q_block, 0)
-    lax.fori_loop(6, 8, q_block, 0)
+    vec_t[2:3, :] = res1[2]
+    vec_s[:, 1, :] = res0[1]
+    vec_s[:, 2, :] = res1[1]
+    row_sums(2, 3)
+    wait_in(xg.at[pl.ds(0, 3), 0], G_SIB2)
+    lax.fori_loop(3, 6, q_block, 0)
 
     wait_in(row_b_in.at[pl.ds(0, TW - 1)], B_ROW)
     row_full1 = jnp.sum(row_b_in[...], axis=0)
@@ -321,8 +379,7 @@
     push_all(TW, tgt_peer, lambda p: sc2_out.at[0], ags_b_in.at[t], B_AGS)
     push_all(ZS, z_peer, lambda p: agz_b.at[z], agz_b.at[z], B_AGZ)
     ags_b_in[t] = sc2_out[0]
-    wait_in(xg.at[pl.ds(0, 3), 0], G_SIB2)
-    lax.fori_loop(3, 6, q_block, 0)
+    col_sums(0, 3)
 
     wait_in(agz_b.at[pl.ds(0, ZS - 1)], B_AGZ)
     wait_in(ags_b_in.at[pl.ds(0, TW - 1)], B_AGS)
@@ -343,75 +400,53 @@
     push_all(SW, src_peer, lambda p: sc_out, sc_in.at[s], C_SRC)
     sc_in[s] = sc_out[...]
 
-    vec_t[0:1, :] = jnp.ones((1, NT), F32)
-    vec_t[1:2, :] = sol2[2]
-    vec_t[2:3, :] = dir1[2]
     vec_t[3:4, :] = res2[2]
-    vec_s[:, 0, :] = jnp.ones((ZS, NS), F32)
-    vec_s[:, 1, :] = sol2[1]
-    vec_s[:, 2, :] = dir1[1]
     vec_s[:, 3, :] = res2[1]
-
-    def fill_stack(points, weights):
-        for v in range(VECS):
-            weight = weights[v:v + 1, :]
-            value = jnp.concatenate([points * weight, jnp.broadcast_to(weight, (16, TILE))], axis=0)
-            high, low = halves(value)
-            stack[v * STACK:(v + 1) * STACK, :] = high
-            stack[(VECS + v) * STACK:(VECS + v + 1) * STACK, :] = low
-
-    def gather_sums(high, low, dims):
-        first = lax.dot_general(stack[...], high, (dims, ((), ())), preferred_element_type=F32)
-        second = lax.dot_general(
-            stack[0:VECS * STACK, :], low, (dims, ((), ())), preferred_element_type=F32
-        )
-        tsum[...] += first[0:VECS * STACK, :] + first[VECS * STACK:, :] + second
-
-    def gradients(points, own, write):
-        ones = tsum[0:64, :], tsum[64:65, :]
-        base = points * ones[1] - ones[0]
-        for v in range(1, VECS):
-            low = v * STACK
-            part = points * tsum[low + 64:low + 65, :] - tsum[low:low + 64, :]
-            weight = own[v] + 1.0 if v == 1 else own[v]
-            write(v - 1, base * weight + part)
-
-    tsum[...] = jnp.zeros_like(tsum)
-
-    def col_step(zz, carry):
-        fill_stack(jnp.concatenate([xg[zz, 0], xg[zz, 1]], axis=0), vec_s[zz])
-        gather_sums(q_hi[zz], q_lo[zz], ((1,), (0,)))
-        return carry
-    lax.fori_loop(0, ZS, col_step, 0)
+    first_step = alpha0 + alpha1 * beta0
+
+    def sums_of(points, out, v):
+        low = v * STACK
+        return points * out[low + 64:low + 65, :] - out[low:low + 64, :]
+
+    def early_gradients(points, out, own, write):
+        ones = sums_of(points, out, 0)
+        zeroth = sums_of(points, out, 1)
+        latest = sums_of(points, out, 2)
+        write(0, (1.0 + first_step * own[0] + alpha1 * own[1]) * ones + first_step * zeroth + alpha1 * latest)
+        write(1, (own[1] + beta0 * own[0]) * ones + latest + beta0 * zeroth)
+
+    def late_gradient(points, out, own, write):
+        write(2, own[2] * sums_of(points, out, 0) + sums_of(points, out, 3))
 
     def write_col(part, value):
         for k in range(XS):
             g_col[part, k] = value[k * 16:(k + 1) * 16, :]
+
+    def write_row(part, value):
+        for k in range(TW):
+            g_row[part, k] = value[k * 8:(k + 1) * 8, :]
+
+    early, late = pl.ds(0, 2), pl.ds(2, 1)
     own_t = vec_t[:, my_tile]
-    gradients(ysub[...], [own_t[v:v + 1, :] for v in range(VECS)], write_col)
-    push_all(XS, x_peer, lambda p: g_col.at[:, lax.rem(x + p, XS)], g_col_in.at[x], D_COL)
+    own_t = [own_t[v:v + 1, :] for v in range(1, VECS)]
+    own_s = [res0[0], res1[0], res2[0]]
+    early_gradients(ysub[...], t_col, own_t, write_col)
+    push_all(XS, x_peer, lambda p: g_col.at[early, lax.rem(x + p, XS)], g_col_in.at[x, early], D_COL)
+    early_gradients(xs, t_row, own_s, write_row)
+    push_all(TW, tgt_peer, lambda p: g_row.at[early, lax.rem(t + p, TW)], g_row_in.at[t, early], D_ROW)
+    col_sums(3, 4)
+    late_gradient(ysub[...], t_col, own_t, write_col)
+    push_all(XS, x_peer, lambda p: g_col.at[late, lax.rem(x + p, XS)], g_col_in.at[x, late], D_COL2)
     g_col_in[x] = g_col[:, x]
+    row_sums(3, 4)
+    late_gradient(xs, t_row, own_s, write_row)
+    push_all(TW, tgt_peer, lambda p: g_row.at[late, lax.rem(t + p, TW)], g_row_in.at[t, late], D_ROW2)
+    g_row_in[t] = g_row[:, t]
 
     wait_in(sc_in.at[pl.ds(0, SW - 1)], C_SRC)
     sc2_out[1] = jnp.sum(sc_in[...], axis=0)
     push_all(TW, tgt_peer, lambda p: sc2_out.at[1], sc2_in.at[t], C_TGT)
     sc2_in[t] = sc2_out[1]
-
-    tsum[...] = jnp.zeros_like(tsum)
-
-    def row_step(n, carry):
-        cs = pl.ds(pl.multiple_of(n * TILE, TILE), TILE)
-        fill_stack(yt_ref[:, cs], vec_t[:, cs])
-        gather_sums(plan_hi[:, cs], plan_lo[:, cs], ((1,), (1,)))
-        return carry
-    lax.fori_loop(0, NT // TILE, row_step, 0)
-
-    def write_row(part, value):
-        for k in range(TW):
-            g_row[part, k] = value[k * 8:(k + 1) * 8, :]
-    gradients(xs, [None, sol2[0], dir1[0], res2[0]], write_row)
-    push_all(TW, tgt_peer, lambda p: g_row.at[:, lax.rem(t + p, TW)], g_row_in.at[t], D_ROW)
-    g_row_in[t] = g_row[:, t]
 
     wait_in(sc2_in.at[pl.ds(0, TW - 1)], C_TGT)
     sums = jnp.sum(sc2_in[...], axis=0)
@@ -423,26 +458,47 @@
     def combine(parts):
         return (parts[0] + both * parts[1] + alpha2 * parts[2]) * (1.0 / EPSILON)
 
-    wait_in(g_col_in.at[pl.ds(0, XS - 1)], D_COL)
+    def lead_of(zz):
+        return pl.ds(pl.multiple_of(zz * TILE, TILE), LEAD)
+
+    def rest_of(zz):
+        return pl.ds(pl.multiple_of(zz * TILE + LEAD, 128), TILE - LEAD)
+
+    wait_in(g_col_in.at[pl.ds(0, XS - 1), early], D_COL)
+    wait_in(g_col_in.at[pl.ds(0, XS - 1), late], D_COL2)
     gt_ref[x, :, my_tile] = combine(jnp.sum(g_col_in[...], axis=0))
-    for dx in range(XS):
-        def step(p, carry):
-            device = (lax.rem(x + dx, XS) * ZS + lax.rem(z + p, ZS), t)
-            push(gt_ref.at[x, :, my_tile], gt_ref.at[x, :, my_tile], O_COL, device, O_X + dx)
-            return carry
-        lax.fori_loop(1 if dx == 0 else 0, ZS, step, 0)
-
-    wait_in(g_row_in.at[pl.ds(0, TW - 1)], D_ROW)
+    mine = gt_ref.at[x, :, rest_of(z)]
+    push_all(XS, x_peer, lambda p: mine, mine, O_XX)
+    for p in (4, 3, ZS - 3, 2, ZS - 2, 1, ZS - 1):
+        push(gt_ref.at[x, :, lead_of(z)], gt_ref.at[x, :, lead_of(z)], O_ZF, z_peer(p), IN_ZF + p)
+
+    def lead_along_x(zz):
+        for p in range(1, XS):
+            push(gt_ref.at[x, :, lead_of(zz)], gt_ref.at[x, :, lead_of(zz)], O_ZF, x_peer(p), IN_XF + p)
+
+    lead_along_x(z)
+
+    wait_in(g_row_in.at[pl.ds(0, TW - 1), early], D_ROW)
+    wait_in(g_row_in.at[pl.ds(0, TW - 1), late], D_ROW2)
     gs_ref[t] = combine(jnp.sum(g_row_in[...], axis=0))
     push_all(TW, tgt_peer, lambda p: gs_ref.at[t], gs_ref.at[t], O_ROW)
 
     sol_src_ref[...] = sol2[0] + both * dir1[0] + alpha2 * res2[0]
     sol_tgt_ref[...] = sol2[2] + both * dir1[2] + alpha2 * res2[2]
 
+    wait_in(gt_ref.at[pl.ds(0, XS - 1), :, pl.ds(0, TILE - LEAD)], O_XX)
+    push_all(
+        ZS, z_peer, lambda p: gt_ref.at[:, :, rest_of(z)], gt_ref.at[:, :, rest_of(z)], O_XZ
+    )
+    for p in (1, ZS - 1, 2, ZS - 2, 3, ZS - 3, 4):
+        zz = lax.rem(z + ZS - p, ZS)
+        wait_in(gt_ref.at[x, :, lead_of(zz)], IN_ZF + p)
+        lead_along_x(zz)
+
     wait_in(gs_ref.at[pl.ds(0, TW - 1)], O_ROW)
-    wait_in(gt_ref.at[x, :, pl.ds(0, (ZS - 1) * TILE)], O_X)
-    for dx in range(1, XS):
-        wait_in(gt_ref.at[lax.rem(x + XS - dx, XS)], O_X + dx)
+    wait_in(gt_ref.at[:, :, pl.ds(0, (ZS - 1) * (TILE - LEAD))], O_XZ)
+    for p in range(1, XS):
+        wait_in(gt_ref.at[0, :, pl.ds(0, ZS * LEAD)], IN_XF + p)
 
     wait_out(col_a_in.at[pl.ds(0, SW - 1)], A_COL)
     wait_out(row_a_in.at[pl.ds(0, TW - 1)], A_ROW)
@@ -457,28 +513,45 @@
     wait_out(ags_b_in.at[pl.ds(0, TW - 1)], B_AGS)
     wait_out(sc_in.at[pl.ds(0, SW - 1)], C_SRC)
     wait_out(sc2_in.at[pl.ds(0, TW - 1)], C_TGT)
-    wait_out(g_row_in.at[pl.ds(0, TW - 1)], D_ROW)
-    wait_out(g_col_in.at[pl.ds(0, XS - 1)], D_COL)
+    wait_out(g_row_in.at[pl.ds(0, TW - 1), early], D_ROW)
+    wait_out(g_col_in.at[pl.ds(0, XS - 1), early], D_COL)
+    wait_out(g_row_in.at[pl.ds(0, TW - 1), late], D_ROW2)
+    wait_out(g_col_in.at[pl.ds(0, XS - 1), late], D_COL2)
     wait_out(gs_ref.at[pl.ds(0, TW - 1)], O_ROW)
-    wait_out(gt_ref.at[pl.ds(0, 3)], O_COL)
-    wait_out(gt_ref.at[0, :, pl.ds(0, (ZS - 1) * TILE)], O_COL)
+    wait_out(gt_ref.at[pl.ds(0, XS - 1), :, pl.ds(0, TILE - LEAD)], O_XX)
+    wait_out(gt_ref.at[:, :, pl.ds(0, (ZS - 1) * (TILE - LEAD))], O_XZ)
+    wait_out(gt_ref.at[pl.ds(0, 3), :, pl.ds(0, ZS * LEAD)], O_ZF)
+    wait_out(gt_ref.at[0, :, pl.ds(0, (ZS - 1) * LEAD)], O_ZF)
     wait_out(xg.at[pl.ds(0, 4), 0], G_NEAR)
     wait_out(xg.at[pl.ds(0, 3), 0], G_FAR)
     wait_out(xg.at[pl.ds(0, 4), 0], G_SIB1)
     wait_out(xg.at[pl.ds(0, 3), 0], G_SIB2)
 
 
+def hand_out(*refs):
+    count = len(refs) // 2
+    sems = refs[-1]
+    copies = [pltpu.make_async_copy(refs[k], refs[count + k], sems.at[k]) for k in range(count)]
+    for copy in copies:
+        copy.start()
+    for copy in copies:
+        copy.wait()
+
+
 def body(src_points, tgt_points, src_potential, tgt_potential, src_rhs, tgt_rhs):
     normalizer = 1.0 / math.sqrt(NS * SW * NT * TW)
     vmem = pl.BlockSpec(memory_space=pltpu.VMEM)
+    far = pl.BlockSpec(memory_space=pltpu.HBM)
 
     def buf(*shape, dtype=F32):
         return pltpu.VMEM(shape, dtype)
 
     scratch = [
+        buf(2, DIM // 2, NS), buf(DIM, NT), buf(1, NS), buf(1, NT), buf(1, NS), buf(1, NT),
+        pltpu.SemaphoreType.DMA((6,)),
         buf(NS, NT), buf(NS, NT, dtype=BF16), buf(NS, NT, dtype=BF16),
         buf(ZS, NS, TILE, dtype=BF16), buf(ZS, NS, TILE, dtype=BF16),
-        buf(NS, 256, dtype=BF16), buf(256, NT, dtype=BF16), buf(NS, TILE),
+        buf(NS, 256, dtype=BF16), buf(256, NT, dtype=BF16),
         buf(NS, 128), buf(NS, 128), buf(NS, 128), buf(NS, 128),
         buf(4, NT), buf(SW, 4, SUB), buf(2, NS), buf(TW, 2, NS),
         buf(2, NS), buf(ZS, 2, NS),
@@ -487,30 +560,39 @@
         buf(1, NT), buf(ZS, 1, NS), buf(TW, 1, 128),
         buf(1, 128), buf(SW, 1, 128), buf(2, 1, 128), buf(TW, 1, 128),
         buf(DIM, TILE), buf(VECS, NT), buf(ZS, VECS, NS),
-        buf(2 * VECS * STACK, TILE, dtype=BF16), buf(VECS * STACK, TILE),
+        buf(2 * 3 * STACK, TILE, dtype=BF16),
+        buf(VECS * STACK, NS), buf(VECS * STACK, TILE),
         buf(3, TW, 8, NS), buf(TW, 3, 8, NS),
         buf(3, XS, 16, TILE), buf(XS, 3, 16, TILE),
         buf(ZS, 2, DIM // 2, NS),
-        pltpu.SemaphoreType.DMA((N_SEMS,)), pltpu.SemaphoreType.DMA((O_X + XS,)),
+        pltpu.SemaphoreType.DMA((N_SEMS,)), pltpu.SemaphoreType.DMA((N_IN,)),
     ]
-    sol_src, sol_tgt, grad_src, grad_tgt = pl.pallas_call(
+    shapes = (
+        jax.ShapeDtypeStruct((1, NS), F32),
+        jax.ShapeDtypeStruct((1, NT), F32),
+        jax.ShapeDtypeStruct((TW, 8, NS), F32),
+        jax.ShapeDtypeStruct((XS, 16, NT), F32),
+    )
+    results = pl.pallas_call(
         functools.partial(kernel, math.log2(normalizer)),
-        out_shape=(
-            jax.ShapeDtypeStruct((1, NS), F32),
-            jax.ShapeDtypeStruct((1, NT), F32),
-            jax.ShapeDtypeStruct((TW, 8, NS), F32),
-            jax.ShapeDtypeStruct((XS, 16, NT), F32),
-        ),
-        in_specs=[vmem] * 6,
+        out_shape=shapes,
+        in_specs=[far] * 6,
         out_specs=[vmem] * 4,
         scratch_shapes=scratch,
         compiler_params=pltpu.CompilerParams(
-            collective_id=1, has_side_effects=True, vmem_limit_bytes=56 * 1024 * 1024
+            collective_id=1, has_side_effects=True, vmem_limit_bytes=60 * 1024 * 1024
         ),
     )(
         src_points.reshape(2, DIM // 2, NS), tgt_points, src_potential.reshape(1, NS),
         tgt_potential.reshape(1, NT), src_rhs.reshape(1, NS), tgt_rhs.reshape(1, NT),
     )
+    sol_src, sol_tgt, grad_src, grad_tgt = pl.pallas_call(
+        hand_out,
+        out_shape=shapes,
+        in_specs=[vmem] * 4,
+        out_specs=[far] * 4,
+        scratch_shapes=[pltpu.SemaphoreType.DMA((4,))],
+    )(*results)
     return (
         sol_src.reshape(NS), sol_tgt.reshape(NT), grad_src.reshape(DIM, NS), grad_tgt.reshape(DIM, NT)
     )

time: 89.1 us -> 76 us (0.85)
  Pallas kernels: 81.6 us -> 74.4 us
  local copies, waits for them, and re-layouts: 5.71 us -> 0 us
    pallas_call x1, Pallas kernels: 81.6 us -> 72.1 us  [body(): pl.pallas_call(functools.partial(kernel, math.log2(normalizer)), out_shap...]
    unnamed x6 -> x0, local copies, waits for them, and re-layouts: 5.71 us -> none
    pallas_call x0 -> x1, Pallas kernels: none -> 2.38 us  [body(): pl.pallas_call(hand_out, out_shape=shapes, in_specs=[vmem] * 4, out_specs...]
where the time goes in v2:
time: 76 us; the launch traced here: 75.1 us
  Pallas kernels  74.4 us (98%)
    pallas_call x1, Pallas kernels, body(): pl.pallas_call(functools.partial(kernel, math.log2(normalizer)), out_shap...  72.1 us
    pallas_call x1, Pallas kernels, body(): pl.pallas_call(hand_out, out_shape=shapes, in_specs=[vmem] * 4, out_specs...  2.38 us

profile of v2, /device:TPU:1, one launch (start us, length us, event | category | flops | bytes accessed | tf_op | source)
XLA Modules:
  0.0 75.1 jit_solution(9353288909811119154)
XLA Ops:
  0.6 72.1 %shard_map.93 = (f32[1,512]{1,0:T(1,128)}, f32[1,4096]{1,0:T(1,128)}, f32[8,8,512]{2,1,0:T(8,128)}, f32[4,16,4096]{2,1,0:T(8,128)}) custom-call(f32[2,32,512]{2,1,0:T(8,128)} %bitcast.9, f32[64,4096]{1,0:T(8,128)} %yt_hbm.1, f32[1,512]{1,0:T(1,128)} %bitcast.12, f32[1,4096]{1,0:T(1,128)} %bitcast.10, f32[1,512]{1,0:T(1,128)} %bitcast.13, f32[1,4096]{1,0:T(1,128)} %bitcast.11), custom_call_target="tpu_custom_call" | custom-call | tf_op jit(solution)/shard_map/pallas_call | solution.py:576
  72.7 2.4 %shard_map.94 = (f32[1,512]{1,0:T(1,128)}, f32[1,4096]{1,0:T(1,128)}, f32[8,8,512]{2,1,0:T(8,128)}, f32[4,16,4096]{2,1,0:T(8,128)}) custom-call(f32[1,512]{1,0:T(1,128)} %get-tuple-element.12.refs_0_, f32[1,4096]{1,0:T(1,128)} %get-tuple-element.13.refs_1_, f32[8,8,512]{2,1,0:T(8,128)} %get-tuple-element.14.refs_2_, f32[4,16,4096]{2,1,0:T(8,128)} %get-tuple-element.15.refs_3_), custom_call_target="tpu_custom_call" | custom-call | tf_op jit(solution)/shard_map/pallas_call | solution.py:589

commit v3 on v2

--- a/solution.py
+++ b/solution.py
@@ -25,10 +25,10 @@
 VECS = 4
 
 (A_COL, A_ROW, A_INIT, A_AGC, A_AGZ, A_AGS, B_COL, B_ROW, B_AGC, B_AGZ, B_AGS, C_SRC, C_TGT,
- D_ROW, D_COL, D_ROW2, D_COL2, O_ROW, O_XX, O_XZ, O_ZF, G_NEAR, G_FAR, G_SIB1, G_SIB2) = range(25)
-IN_ZF = 25
+ D_ROW, D_COL, D_ROW2, D_COL2, O_ROW, O_XX, O_XZ, O_ZF, G_RING1, G_RING2, G_RING3, G_RING4, G_SIB1, G_SIB2) = range(27)
+IN_ZF = 27
 IN_XF = IN_ZF + ZS
-N_SEMS = 25
+N_SEMS = 27
 N_IN = IN_XF + XS
 LEAD = 384
 
@@ -138,7 +138,7 @@
 
     greet(SW, src_peer)
     greet(TW, tgt_peer)
-    for copy in loads:
+    for copy in loads[1:]:
         copy.wait()
 
     xs = jnp.concatenate([xs_ref[0], xs_ref[1]], axis=0)
@@ -153,24 +153,23 @@
 
     x4t[...] = x_parts(xs)
 
-    def y_step(n, carry):
+    fcol[...] = across(f_ref[...] * LOG2E + shift)
+    acol[...] = across(a0)
+    racc[...] = jnp.zeros_like(racc)
+    racc2[...] = jnp.zeros_like(racc2)
+
+    loads[0].wait()
+
+    def plan_step(n, carry):
         cs = pl.ds(pl.multiple_of(n * TILE, TILE), TILE)
         high, low = halves(yt_ref[:, cs])
         y4[0:64, cs] = high
         y4[64:128, cs] = low
         y4[128:192, cs] = high
         y4[192:256, cs] = low
-        return carry
-    lax.fori_loop(0, NT // TILE, y_step, 0)
-
-    fcol[...] = across(f_ref[...] * LOG2E + shift)
-    acol[...] = across(a0)
-    racc[...] = jnp.zeros_like(racc)
-    racc2[...] = jnp.zeros_like(racc2)
-
-    def plan_step(n, carry):
-        cs = pl.ds(pl.multiple_of(n * TILE, TILE), TILE)
-        cross = jnp.dot(x4t[...], y4[:, cs], preferred_element_type=F32)
+        cross = jnp.dot(
+            x4t[...], jnp.concatenate([high, low, high, low], axis=0), preferred_element_type=F32
+        )
         g_now = g_ref[:, cs] * LOG2E
         b_now = b0_ref[:, cs]
         mass_sum = jnp.zeros((8, TILE), F32)
@@ -208,8 +207,8 @@
     push_all(SW, src_peer, lambda p: col_a.at[:, sub_of(p)], col_a_in.at[s], A_COL)
     push_all(TW, tgt_peer, lambda p: row_a, row_a_in.at[t], A_ROW)
     push_all(ZS, z_peer, lambda p: init_out, init_in.at[z], A_INIT)
-    for p in (1, ZS - 1, 2, ZS - 2):
-        push(xs_ref.at[core], xg.at[z, core], G_NEAR, z_peer(p))
+    push(xs_ref.at[core], xg.at[z, core], G_RING1, z_peer(1))
+    push(xs_ref.at[core], xg.at[z, core], G_RING1, z_peer(ZS - 1))
     col_a_in[s] = col_a[:, my_sub]
     row_a_in[t] = row_a[...]
     init_in[z] = init_out[...]
@@ -230,6 +229,11 @@
             q_hi[zz, r:r + 64, :] = high
             q_lo[zz, r:r + 64, :] = low
         return carry
+
+    def pass_on(p, k):
+        before, after = lax.rem(z + ZS - p, ZS), lax.rem(z + p, ZS)
+        push(xg.at[before, core], xg.at[before, core], k, z_peer(1))
+        push(xg.at[after, core], xg.at[after, core], k, z_peer(ZS - 1))
 
     def fill_stack(points, weights):
         count = len(weights)
@@ -262,15 +266,16 @@
             return carry
         lax.fori_loop(0, NT // TILE, step, 0)
 
-    def col_sums(low, high):
-        def step(zz, carry):
+    def col_sums(low, high, first=0, last=ZS):
+        def step(p, carry):
+            zz = lax.rem(z + p, ZS)
             fill_stack(
                 jnp.concatenate([xg[zz, 0], xg[zz, 1]], axis=0),
                 [vec_s[zz, v:v + 1, :] for v in range(low, high)],
             )
             add_sums(t_col, low, high - low, q_hi[zz], q_lo[zz], ((1,), (0,)))
             return carry
-        lax.fori_loop(0, ZS, step, 0)
+        lax.fori_loop(first, last, step, 0)
 
     t_row[...] = jnp.zeros_like(t_row)
     t_col[...] = jnp.zeros_like(t_col)
@@ -278,6 +283,8 @@
     vec_t[1:2, :] = b0
     vec_s[:, 0, :] = jnp.ones((ZS, NS), F32)
     row_sums(0, 2, split=True)
+    wait_in(xg.at[pl.ds(0, 2), 0], G_RING1)
+    pass_on(1, G_RING2)
 
     wait_in(row_a_in.at[pl.ds(0, TW - 1)], A_ROW)
     row_full = jnp.sum(row_a_in[...], axis=0)
@@ -293,12 +300,11 @@
     push_all(ZS, z_peer, lambda p: agz_a.at[z], agz_a.at[z], A_AGZ)
     ags_a_in[t] = ags_a[...]
     wait_in(init_in.at[pl.ds(0, ZS - 1)], A_INIT)
-    wait_in(xg.at[pl.ds(0, 4), 0], G_NEAR)
+    wait_in(xg.at[pl.ds(0, 2), 0], G_RING2)
+    pass_on(2, G_RING3)
     for p in (1, ZS - 1, 2, ZS - 2):
         zz = lax.rem(z + p, ZS)
         push(xg.at[zz, core], xg.at[zz, core], G_SIB1, sibling)
-    for p in (3, ZS - 3, 4):
-        push(xs_ref.at[core], xg.at[z, core], G_FAR, z_peer(p))
     q_block(0, 0)
     wait_in(xg.at[pl.ds(0, 4), 0], G_SIB1)
     lax.fori_loop(1, 3, q_block, 0)
@@ -356,16 +362,21 @@
     push_all(TW, tgt_peer, lambda p: row_b, row_b_in.at[t], B_ROW)
     col_b_in[s] = col_b[:, my_sub]
     row_b_in[t] = row_b[...]
-    wait_in(xg.at[pl.ds(0, 3), 0], G_FAR)
-    for p in (3, ZS - 3, 4):
-        zz = lax.rem(z + p, ZS)
-        push(xg.at[zz, core], xg.at[zz, core], G_SIB2, sibling)
+    wait_in(xg.at[pl.ds(0, 2), 0], G_RING3)
+    before, after = lax.rem(z + ZS - 3, ZS), lax.rem(z + 3, ZS)
+    top, rest = pl.ds(0, 16), pl.ds(16, 16)
+    push(xg.at[before, core, top], xg.at[before, core, top], G_RING4, z_peer(1))
+    push(xg.at[after, core, rest], xg.at[after, core, rest], G_RING4, z_peer(ZS - 1))
     vec_t[2:3, :] = res1[2]
     vec_s[:, 1, :] = res0[1]
     vec_s[:, 2, :] = res1[1]
     row_sums(2, 3)
-    wait_in(xg.at[pl.ds(0, 3), 0], G_SIB2)
-    lax.fori_loop(3, 6, q_block, 0)
+    col_sums(0, 3, 0, 3)
+    col_sums(0, 3, 6, 8)
+    wait_in(xg.at[0, 0], G_RING4)
+    for p in (3, ZS - 3, 4):
+        zz = lax.rem(z + p, ZS)
+        push(xg.at[zz, core], xg.at[zz, core], G_SIB2, sibling)
 
     wait_in(row_b_in.at[pl.ds(0, TW - 1)], B_ROW)
     row_full1 = jnp.sum(row_b_in[...], axis=0)
@@ -379,7 +390,9 @@
     push_all(TW, tgt_peer, lambda p: sc2_out.at[0], ags_b_in.at[t], B_AGS)
     push_all(ZS, z_peer, lambda p: agz_b.at[z], agz_b.at[z], B_AGZ)
     ags_b_in[t] = sc2_out[0]
-    col_sums(0, 3)
+    wait_in(xg.at[pl.ds(0, 3), 0], G_SIB2)
+    lax.fori_loop(3, 6, q_block, 0)
+    col_sums(0, 3, 3, 6)
 
     wait_in(agz_b.at[pl.ds(0, ZS - 1)], B_AGZ)
     wait_in(ags_b_in.at[pl.ds(0, TW - 1)], B_AGS)
@@ -438,15 +451,15 @@
     late_gradient(ysub[...], t_col, own_t, write_col)
     push_all(XS, x_peer, lambda p: g_col.at[late, lax.rem(x + p, XS)], g_col_in.at[x, late], D_COL2)
     g_col_in[x] = g_col[:, x]
+    wait_in(sc_in.at[pl.ds(0, SW - 1)], C_SRC)
+    sc2_out[1] = jnp.sum(sc_in[...], axis=0)
+    push_all(TW, tgt_peer, lambda p: sc2_out.at[1], sc2_in.at[t], C_TGT)
+    sc2_in[t] = sc2_out[1]
+
     row_sums(3, 4)
     late_gradient(xs, t_row, own_s, write_row)
     push_all(TW, tgt_peer, lambda p: g_row.at[late, lax.rem(t + p, TW)], g_row_in.at[t, late], D_ROW2)
     g_row_in[t] = g_row[:, t]
-
-    wait_in(sc_in.at[pl.ds(0, SW - 1)], C_SRC)
-    sc2_out[1] = jnp.sum(sc_in[...], axis=0)
-    push_all(TW, tgt_peer, lambda p: sc2_out.at[1], sc2_in.at[t], C_TGT)
-    sc2_in[t] = sc2_out[1]
 
     wait_in(sc2_in.at[pl.ds(0, TW - 1)], C_TGT)
     sums = jnp.sum(sc2_in[...], axis=0)
@@ -469,7 +482,7 @@
     gt_ref[x, :, my_tile] = combine(jnp.sum(g_col_in[...], axis=0))
     mine = gt_ref.at[x, :, rest_of(z)]
     push_all(XS, x_peer, lambda p: mine, mine, O_XX)
-    for p in (4, 3, ZS - 3, 2, ZS - 2, 1, ZS - 1):
+    for p in (1, ZS - 1, 2, ZS - 2, 3, ZS - 3, 4):
         push(gt_ref.at[x, :, lead_of(z)], gt_ref.at[x, :, lead_of(z)], O_ZF, z_peer(p), IN_ZF + p)
 
     def lead_along_x(zz):
@@ -477,11 +490,6 @@
             push(gt_ref.at[x, :, lead_of(zz)], gt_ref.at[x, :, lead_of(zz)], O_ZF, x_peer(p), IN_XF + p)
 
     lead_along_x(z)
-
-    wait_in(g_row_in.at[pl.ds(0, TW - 1), early], D_ROW)
-    wait_in(g_row_in.at[pl.ds(0, TW - 1), late], D_ROW2)
-    gs_ref[t] = combine(jnp.sum(g_row_in[...], axis=0))
-    push_all(TW, tgt_peer, lambda p: gs_ref.at[t], gs_ref.at[t], O_ROW)
 
     sol_src_ref[...] = sol2[0] + both * dir1[0] + alpha2 * res2[0]
     sol_tgt_ref[...] = sol2[2] + both * dir1[2] + alpha2 * res2[2]
@@ -494,6 +502,11 @@
         zz = lax.rem(z + ZS - p, ZS)
         wait_in(gt_ref.at[x, :, lead_of(zz)], IN_ZF + p)
         lead_along_x(zz)
+        if p == ZS - 1:
+            wait_in(g_row_in.at[pl.ds(0, TW - 1), early], D_ROW)
+            wait_in(g_row_in.at[pl.ds(0, TW - 1), late], D_ROW2)
+            gs_ref[t] = combine(jnp.sum(g_row_in[...], axis=0))
+            push_all(TW, tgt_peer, lambda p: gs_ref.at[t], gs_ref.at[t], O_ROW)
 
     wait_in(gs_ref.at[pl.ds(0, TW - 1)], O_ROW)
     wait_in(gt_ref.at[:, :, pl.ds(0, (ZS - 1) * (TILE - LEAD))], O_XZ)
@@ -522,8 +535,9 @@
     wait_out(gt_ref.at[:, :, pl.ds(0, (ZS - 1) * (TILE - LEAD))], O_XZ)
     wait_out(gt_ref.at[pl.ds(0, 3), :, pl.ds(0, ZS * LEAD)], O_ZF)
     wait_out(gt_ref.at[0, :, pl.ds(0, (ZS - 1) * LEAD)], O_ZF)
-    wait_out(xg.at[pl.ds(0, 4), 0], G_NEAR)
-    wait_out(xg.at[pl.ds(0, 3), 0], G_FAR)
+    for k in (G_RING1, G_RING2, G_RING3):
+        wait_out(xg.at[pl.ds(0, 2), 0], k)
+    wait_out(xg.at[0, 0], G_RING4)
     wait_out(xg.at[pl.ds(0, 4), 0], G_SIB1)
     wait_out(xg.at[pl.ds(0, 3), 0], G_SIB2)
 

time: 76 us -> 69.4 us (0.913); the launches traced: 75.1 us -> 69.3 us
  Pallas kernels: 74.4 us -> 68.6 us
    pallas_call x1, Pallas kernels: 72.1 us -> 66.3 us  [body(): pl.pallas_call(functools.partial(kernel, math.log2(normalizer)), out_shap...]
where the time goes in v3:
time: 69.4 us; the launch traced here: 69.3 us
  Pallas kernels  68.6 us (99%)
    pallas_call x1, Pallas kernels, body(): pl.pallas_call(functools.partial(kernel, math.log2(normalizer)), out_shap...  66.3 us
    pallas_call x1, Pallas kernels, body(): pl.pallas_call(hand_out, out_shape=shapes, in_specs=[vmem] * 4, out_specs...  2.38 us

profile of v3, /device:TPU:1, one launch (start us, length us, event | category | flops | bytes accessed | tf_op | source)
XLA Modules:
  0.0 69.3 jit_solution(13813759911227426809)
XLA Ops:
  0.6 66.3 %shard_map.93 = (f32[1,512]{1,0:T(1,128)}, f32[1,4096]{1,0:T(1,128)}, f32[8,8,512]{2,1,0:T(8,128)}, f32[4,16,4096]{2,1,0:T(8,128)}) custom-call(f32[2,32,512]{2,1,0:T(8,128)} %bitcast.9, f32[64,4096]{1,0:T(8,128)} %yt_hbm.1, f32[1,512]{1,0:T(1,128)} %bitcast.12, f32[1,4096]{1,0:T(1,128)} %bitcast.10, f32[1,512]{1,0:T(1,128)} %bitcast.13, f32[1,4096]{1,0:T(1,128)} %bitcast.11), custom_call_target="tpu_custom_call" | custom-call | tf_op jit(solution)/shard_map/pallas_call | solution.py:590
  66.9 2.4 %shard_map.94 = (f32[1,512]{1,0:T(1,128)}, f32[1,4096]{1,0:T(1,128)}, f32[8,8,512]{2,1,0:T(8,128)}, f32[4,16,4096]{2,1,0:T(8,128)}) custom-call(f32[1,512]{1,0:T(1,128)} %get-tuple-element.12.refs_0_, f32[1,4096]{1,0:T(1,128)} %get-tuple-element.13.refs_1_, f32[8,8,512]{2,1,0:T(8,128)} %get-tuple-element.14.refs_2_, f32[4,16,4096]{2,1,0:T(8,128)} %get-tuple-element.15.refs_3_), custom_call_target="tpu_custom_call" | custom-call | tf_op jit(solution)/shard_map/pallas_call | solution.py:603

commit v4 on v3

--- a/solution.py
+++ b/solution.py
@@ -21,14 +21,16 @@
 NS, NT = 512, 4096
 SUB = NT // SW
 TILE = 512
+STEP = 128
+ROWS = 64
 STACK = 80
 VECS = 4
 
 (A_COL, A_ROW, A_INIT, A_AGC, A_AGZ, A_AGS, B_COL, B_ROW, B_AGC, B_AGZ, B_AGS, C_SRC, C_TGT,
- D_ROW, D_COL, D_ROW2, D_COL2, O_ROW, O_XX, O_XZ, O_ZF, G_RING1, G_RING2, G_RING3, G_RING4, G_SIB1, G_SIB2) = range(27)
-IN_ZF = 27
+ D_ROW, D_COL, D_ROW2, D_COL2, O_ROW, O_XX, O_XZ, O_ZF, G_NEAR, G_FAR, G_SIB1, G_SIB2) = range(25)
+IN_ZF = 25
 IN_XF = IN_ZF + ZS
-N_SEMS = 27
+N_SEMS = 25
 N_IN = IN_XF + XS
 LEAD = 384
 
@@ -50,21 +52,19 @@
     return jnp.concatenate([block] * times, axis=1)
 
 
-def total(value):
-    return jnp.sum(jnp.sum(value, axis=1, keepdims=True), axis=0, keepdims=True)
-
-
-def lanes(*values):
-    spot = lax.broadcasted_iota(jnp.int32, (1, 128), 1)
-    row = jnp.zeros((1, 128), F32)
-    for index, value in enumerate(values):
-        row = row + jnp.where(spot == index, value, 0.0)
-    return row
-
-
-def lane(row, index):
-    spot = lax.broadcasted_iota(jnp.int32, (1, 128), 1)
-    return jnp.sum(jnp.where(spot == index, row, 0.0), axis=1, keepdims=True)
+def lane_tiles(value):
+    parts = [value[:, k:k + 128] for k in range(0, value.shape[1], 128)]
+    while len(parts) > 1:
+        parts = [parts[k] + parts[k + 1] for k in range(0, len(parts), 2)]
+    return parts[0]
+
+
+def fold(vector):
+    return lane_tiles(vector)
+
+
+def across_lanes(rows):
+    return jnp.sum(rows, axis=1, keepdims=True)
 
 
 def kernel(
@@ -161,32 +161,27 @@
     loads[0].wait()
 
     def plan_step(n, carry):
-        cs = pl.ds(pl.multiple_of(n * TILE, TILE), TILE)
+        cs = pl.ds(pl.multiple_of(n * STEP, STEP), STEP)
         high, low = halves(yt_ref[:, cs])
-        y4[0:64, cs] = high
-        y4[64:128, cs] = low
-        y4[128:192, cs] = high
-        y4[192:256, cs] = low
-        cross = jnp.dot(
-            x4t[...], jnp.concatenate([high, low, high, low], axis=0), preferred_element_type=F32
-        )
+        parts = jnp.concatenate([high, low, high, low], axis=0)
+        y4[:, cs] = parts
+        cross = jnp.dot(x4t[...], parts, preferred_element_type=F32)
         g_now = g_ref[:, cs] * LOG2E
         b_now = b0_ref[:, cs]
-        mass_sum = jnp.zeros((8, TILE), F32)
-        a_sum = jnp.zeros((8, TILE), F32)
-        for r in range(0, NS, 64):
-            p = jnp.exp2(cross[r:r + 64, :] + tiled(fcol[r:r + 64, :], 4) + g_now)
-            plan[r:r + 64, cs] = p
-            racc[r:r + 64, :] += (p[:, 0:128] + p[:, 128:256]) + (p[:, 256:384] + p[:, 384:512])
-            pb = p * b_now
-            racc2[r:r + 64, :] += (pb[:, 0:128] + pb[:, 128:256]) + (pb[:, 256:384] + pb[:, 384:512])
-            pa = p * tiled(acol[r:r + 64, :], 4)
-            mass_sum = mass_sum + jnp.sum(p.reshape(8, 8, TILE), axis=0)
-            a_sum = a_sum + jnp.sum(pa.reshape(8, 8, TILE), axis=0)
+        mass_sum = jnp.zeros((8, STEP), F32)
+        a_sum = jnp.zeros((8, STEP), F32)
+        for r in range(0, NS, ROWS):
+            p = jnp.exp2(cross[r:r + ROWS, :] + tiled(fcol[r:r + ROWS, :], STEP // 128) + g_now)
+            plan[r:r + ROWS, cs] = p
+            racc[r:r + ROWS, :] += lane_tiles(p)
+            racc2[r:r + ROWS, :] += lane_tiles(p * b_now)
+            pa = p * tiled(acol[r:r + ROWS, :], STEP // 128)
+            mass_sum = mass_sum + jnp.sum(p.reshape(ROWS // 8, 8, STEP), axis=0)
+            a_sum = a_sum + jnp.sum(pa.reshape(ROWS // 8, 8, STEP), axis=0)
         col_a[0:1, cs] = jnp.sum(mass_sum, axis=0, keepdims=True)
         col_a[1:2, cs] = jnp.sum(a_sum, axis=0, keepdims=True)
         return carry
-    lax.fori_loop(0, NT // TILE, plan_step, 0)
+    lax.fori_loop(0, NT // STEP, plan_step, 0, unroll=2)
 
     mass_part = along(racc[...])
     v_part = along(racc2[...])
@@ -194,21 +189,21 @@
     row_a[1:2, :] = v_part
     init_out[0:1, :] = f_ref[...]
     init_out[1:2, :] = a0
-    norm_part = total(a0 * a0) * (1.0 / TW) + total(b0 * b0) * (1.0 / SW)
+    norm_part = fold(a0 * a0) * (1.0 / TW) + fold(b0 * b0) * (1.0 / SW)
     quad_part = (
-        norm_part * REGULARIZER
-        + total(a0 * a0 * mass_part) + total(b0 * b0 * col_a[0:1, :]) + 2.0 * total(a0 * v_part)
+        norm_part * REGULARIZER + fold(a0 * (a0 * mass_part + 2.0 * v_part))
+        + fold(b0 * b0 * col_a[0:1, :])
     )
-    col_a[2:3, :] = tiled(lanes(norm_part, quad_part), SW)
-    col_a[3:4, :] = jnp.zeros((1, NT), F32)
+    col_a[2:3, :] = tiled(norm_part, SW)
+    col_a[3:4, :] = tiled(quad_part, SW)
 
     pl.semaphore_wait(barrier, SW - 1 + TW - 1)
 
     push_all(SW, src_peer, lambda p: col_a.at[:, sub_of(p)], col_a_in.at[s], A_COL)
     push_all(TW, tgt_peer, lambda p: row_a, row_a_in.at[t], A_ROW)
     push_all(ZS, z_peer, lambda p: init_out, init_in.at[z], A_INIT)
-    push(xs_ref.at[core], xg.at[z, core], G_RING1, z_peer(1))
-    push(xs_ref.at[core], xg.at[z, core], G_RING1, z_peer(ZS - 1))
+    for p in (1, ZS - 1, 2, ZS - 2):
+        push(xs_ref.at[core], xg.at[z, core], G_NEAR, z_peer(p))
     col_a_in[s] = col_a[:, my_sub]
     row_a_in[t] = row_a[...]
     init_in[z] = init_out[...]
@@ -222,18 +217,16 @@
         zz = lax.rem(z + p, ZS)
         points = jnp.concatenate([xg[zz, 0], xg[zz, 1]], axis=0)
         fcol[...] = across(init_in[zz][0:1, :] * LOG2E + shift)
-        cross = jnp.dot(x_parts(points), y4[:, my_tile], preferred_element_type=F32)
-        for r in range(0, NS, 64):
-            value = jnp.exp2(cross[r:r + 64, :] + tiled(fcol[r:r + 64, :], 4) + g_sub)
-            high, low = halves(value)
-            q_hi[zz, r:r + 64, :] = high
-            q_lo[zz, r:r + 64, :] = low
+        parts = x_parts(points)
+        for c in range(0, TILE, 128):
+            some = pl.ds(pl.multiple_of(z * TILE + c, 128), 128)
+            cross = jnp.dot(parts, y4[:, some], preferred_element_type=F32)
+            for r in range(0, NS, 64):
+                value = jnp.exp2(cross[r:r + 64, :] + fcol[r:r + 64, :] + g_sub[:, c:c + 128])
+                high, low = halves(value)
+                q_hi[zz, r:r + 64, c:c + 128] = high
+                q_lo[zz, r:r + 64, c:c + 128] = low
         return carry
-
-    def pass_on(p, k):
-        before, after = lax.rem(z + ZS - p, ZS), lax.rem(z + p, ZS)
-        push(xg.at[before, core], xg.at[before, core], k, z_peer(1))
-        push(xg.at[after, core], xg.at[after, core], k, z_peer(ZS - 1))
 
     def fill_stack(points, weights):
         count = len(weights)
@@ -283,8 +276,6 @@
     vec_t[1:2, :] = b0
     vec_s[:, 0, :] = jnp.ones((ZS, NS), F32)
     row_sums(0, 2, split=True)
-    wait_in(xg.at[pl.ds(0, 2), 0], G_RING1)
-    pass_on(1, G_RING2)
 
     wait_in(row_a_in.at[pl.ds(0, TW - 1)], A_ROW)
     row_full = jnp.sum(row_a_in[...], axis=0)
@@ -292,7 +283,7 @@
     wait_in(col_a_in.at[pl.ds(0, SW - 1)], A_COL)
     col_full = jnp.sum(col_a_in[...], axis=0)
     agc_a[:, my_sub] = col_full[0:2, :]
-    ags_a[...] = col_full[2:3, :]
+    ags_a[...] = col_full[2:4, :]
     agz_a[z] = agz_own
 
     push_all(SW, src_peer, lambda p: agc_a.at[:, my_sub], agc_a.at[:, my_sub], A_AGC)
@@ -300,8 +291,13 @@
     push_all(ZS, z_peer, lambda p: agz_a.at[z], agz_a.at[z], A_AGZ)
     ags_a_in[t] = ags_a[...]
     wait_in(init_in.at[pl.ds(0, ZS - 1)], A_INIT)
-    wait_in(xg.at[pl.ds(0, 2), 0], G_RING2)
-    pass_on(2, G_RING3)
+    wait_in(xg.at[pl.ds(0, 4), 0], G_NEAR)
+    before, after = lax.rem(z + ZS - 2, ZS), lax.rem(z + 2, ZS)
+    top, rest = pl.ds(0, 16), pl.ds(16, 16)
+    push(xg.at[before, core], xg.at[before, core], G_FAR, z_peer(1))
+    push(xg.at[after, core], xg.at[after, core], G_FAR, z_peer(ZS - 1))
+    push(xg.at[before, core, top], xg.at[before, core, top], G_FAR, z_peer(2))
+    push(xg.at[after, core, rest], xg.at[after, core, rest], G_FAR, z_peer(ZS - 2))
     for p in (1, ZS - 1, 2, ZS - 2):
         zz = lax.rem(z + p, ZS)
         push(xg.at[zz, core], xg.at[zz, core], G_SIB1, sibling)
@@ -314,8 +310,8 @@
     wait_in(ags_a_in.at[pl.ds(0, TW - 1)], A_AGS)
     wait_in(agc_a.at[:, pl.ds(0, (SW - 1) * SUB)], A_AGC)
     sums = jnp.sum(ags_a_in[...], axis=0)
-    norm0 = lane(sums, 0)
-    alpha0 = norm0 / lane(sums, 1)
+    norm0 = across_lanes(sums[0:1, :])
+    alpha0 = norm0 / across_lanes(sums[1:2, :])
 
     diag = [row_full[0:1, :] + REGULARIZER, agz_a[:, 0, :] + REGULARIZER, agc_a[0:1, :] + REGULARIZER]
     res0 = [a0, init_in[:, 1, :], b0]
@@ -346,37 +342,34 @@
         return along(racc[...] + racc2[...])
 
     def scalars(res, row_part):
-        norm = total(res[0] * res[0]) * (1.0 / TW) + total(res[2] * res[2]) * (1.0 / SW)
+        norm = fold(res[0] * res[0]) * (1.0 / TW) + fold(res[2] * res[2]) * (1.0 / SW)
         quad = (
-            total(res[0] * res[0] * diag[0]) * (1.0 / TW)
-            + total(res[2] * res[2] * diag[2]) * (1.0 / SW)
-            + 2.0 * total(res[0] * row_part)
+            fold(res[0] * (res[0] * diag[0] * (1.0 / TW) + 2.0 * row_part))
+            + fold(res[2] * res[2] * diag[2]) * (1.0 / SW)
         )
-        return lanes(norm, quad)
+        return norm, quad
 
     row_part = matvec(res1[0], res1[2], True)
     row_b[...] = row_part
-    col_b[1:2, :] = tiled(scalars(res1, row_part), SW)
+    norm_part, quad_part = scalars(res1, row_part)
+    col_b[1:2, :] = tiled(norm_part, SW)
+    col_b[2:3, :] = tiled(quad_part, SW)
+    col_b[3:4, :] = jnp.zeros((1, NT), F32)
 
     push_all(SW, src_peer, lambda p: col_b.at[:, sub_of(p)], col_b_in.at[s], B_COL)
     push_all(TW, tgt_peer, lambda p: row_b, row_b_in.at[t], B_ROW)
     col_b_in[s] = col_b[:, my_sub]
     row_b_in[t] = row_b[...]
-    wait_in(xg.at[pl.ds(0, 2), 0], G_RING3)
-    before, after = lax.rem(z + ZS - 3, ZS), lax.rem(z + 3, ZS)
-    top, rest = pl.ds(0, 16), pl.ds(16, 16)
-    push(xg.at[before, core, top], xg.at[before, core, top], G_RING4, z_peer(1))
-    push(xg.at[after, core, rest], xg.at[after, core, rest], G_RING4, z_peer(ZS - 1))
     vec_t[2:3, :] = res1[2]
     vec_s[:, 1, :] = res0[1]
     vec_s[:, 2, :] = res1[1]
     row_sums(2, 3)
-    col_sums(0, 3, 0, 3)
-    col_sums(0, 3, 6, 8)
-    wait_in(xg.at[0, 0], G_RING4)
+    wait_in(xg.at[pl.ds(0, 3), 0], G_FAR)
     for p in (3, ZS - 3, 4):
         zz = lax.rem(z + p, ZS)
         push(xg.at[zz, core], xg.at[zz, core], G_SIB2, sibling)
+    col_sums(0, 3, 0, 3)
+    col_sums(0, 3, 6, 8)
 
     wait_in(row_b_in.at[pl.ds(0, TW - 1)], B_ROW)
     row_full1 = jnp.sum(row_b_in[...], axis=0)
@@ -384,7 +377,7 @@
     wait_in(col_b_in.at[pl.ds(0, SW - 1)], B_COL)
     col_full1 = jnp.sum(col_b_in[...], axis=0)
     agc_b[:, my_sub] = col_full1[0:1, :]
-    sc2_out[0] = col_full1[1:2, :]
+    sc2_out[0] = col_full1[1:3, :]
 
     push_all(SW, src_peer, lambda p: agc_b.at[:, my_sub], agc_b.at[:, my_sub], B_AGC)
     push_all(TW, tgt_peer, lambda p: sc2_out.at[0], ags_b_in.at[t], B_AGS)
@@ -398,9 +391,9 @@
     wait_in(ags_b_in.at[pl.ds(0, TW - 1)], B_AGS)
     wait_in(agc_b.at[:, pl.ds(0, (SW - 1) * SUB)], B_AGC)
     sums = jnp.sum(ags_b_in[...], axis=0)
-    norm1 = lane(sums, 0)
+    norm1 = across_lanes(sums[0:1, :])
     beta0 = norm1 / norm0
-    alpha1 = norm1 / (lane(sums, 1) - beta0 * norm1 / alpha0)
+    alpha1 = norm1 / (across_lanes(sums[1:2, :]) - beta0 * norm1 / alpha0)
     prod1 = [row_full1, agz_b[:, 0, :], agc_b[...]]
     dir1 = [r1 + beta0 * r0 for r1, r0 in zip(res1, res0)]
     image1 = [d * r + v + beta0 * i for d, r, v, i in zip(diag, res1, prod1, image0)]
@@ -408,7 +401,9 @@
     sol2 = [alpha0 * r0 + alpha1 * d1 for r0, d1 in zip(res0, dir1)]
 
     row_part = matvec(res2[0], res2[2], False)
-    sc_out[...] = scalars(res2, row_part)
+    norm_part, quad_part = scalars(res2, row_part)
+    sc_out[0:1, :] = norm_part
+    sc_out[1:2, :] = quad_part
 
     push_all(SW, src_peer, lambda p: sc_out, sc_in.at[s], C_SRC)
     sc_in[s] = sc_out[...]
@@ -463,9 +458,9 @@
 
     wait_in(sc2_in.at[pl.ds(0, TW - 1)], C_TGT)
     sums = jnp.sum(sc2_in[...], axis=0)
-    norm2 = lane(sums, 0)
+    norm2 = across_lanes(sums[0:1, :])
     beta1 = norm2 / norm1
-    alpha2 = norm2 / (lane(sums, 1) - beta1 * norm2 / alpha1)
+    alpha2 = norm2 / (across_lanes(sums[1:2, :]) - beta1 * norm2 / alpha1)
     both = alpha2 * beta1
 
     def combine(parts):
@@ -535,21 +530,28 @@
     wait_out(gt_ref.at[:, :, pl.ds(0, (ZS - 1) * (TILE - LEAD))], O_XZ)
     wait_out(gt_ref.at[pl.ds(0, 3), :, pl.ds(0, ZS * LEAD)], O_ZF)
     wait_out(gt_ref.at[0, :, pl.ds(0, (ZS - 1) * LEAD)], O_ZF)
-    for k in (G_RING1, G_RING2, G_RING3):
-        wait_out(xg.at[pl.ds(0, 2), 0], k)
-    wait_out(xg.at[0, 0], G_RING4)
+    wait_out(xg.at[pl.ds(0, 4), 0], G_NEAR)
+    wait_out(xg.at[pl.ds(0, 3), 0], G_FAR)
     wait_out(xg.at[pl.ds(0, 4), 0], G_SIB1)
     wait_out(xg.at[pl.ds(0, 3), 0], G_SIB2)
 
 
 def hand_out(*refs):
-    count = len(refs) // 2
     sems = refs[-1]
-    copies = [pltpu.make_async_copy(refs[k], refs[count + k], sems.at[k]) for k in range(count)]
-    for copy in copies:
-        copy.start()
-    for copy in copies:
-        copy.wait()
+    parts = [(refs[3].at[k], refs[7].at[k], refs[11].at[k]) for k in range(XS)]
+    parts += [(refs[k], refs[4 + k], refs[8 + k]) for k in (2, 1, 0)]
+    loads = [pltpu.make_async_copy(src, near, sems.at[k]) for k, (src, _, near) in enumerate(parts)]
+    stores = [
+        pltpu.make_async_copy(near, dst, sems.at[len(parts) + k])
+        for k, (_, dst, near) in enumerate(parts)
+    ]
+    for load in loads:
+        load.start()
+    for load, store in zip(loads, stores):
+        load.wait()
+        store.start()
+    for store in stores:
+        store.wait()
 
 
 def body(src_points, tgt_points, src_potential, tgt_potential, src_rhs, tgt_rhs):
@@ -569,10 +571,10 @@
         buf(NS, 128), buf(NS, 128), buf(NS, 128), buf(NS, 128),
         buf(4, NT), buf(SW, 4, SUB), buf(2, NS), buf(TW, 2, NS),
         buf(2, NS), buf(ZS, 2, NS),
-        buf(2, NT), buf(ZS, 2, NS), buf(1, 128), buf(TW, 1, 128),
-        buf(2, NT), buf(SW, 2, SUB), buf(1, NS), buf(TW, 1, NS),
-        buf(1, NT), buf(ZS, 1, NS), buf(TW, 1, 128),
-        buf(1, 128), buf(SW, 1, 128), buf(2, 1, 128), buf(TW, 1, 128),
+        buf(2, NT), buf(ZS, 2, NS), buf(2, 128), buf(TW, 2, 128),
+        buf(4, NT), buf(SW, 4, SUB), buf(1, NS), buf(TW, 1, NS),
+        buf(1, NT), buf(ZS, 1, NS), buf(TW, 2, 128),
+        buf(2, 128), buf(SW, 2, 128), buf(2, 2, 128), buf(TW, 2, 128),
         buf(DIM, TILE), buf(VECS, NT), buf(ZS, VECS, NS),
         buf(2 * 3 * STACK, TILE, dtype=BF16),
         buf(VECS * STACK, NS), buf(VECS * STACK, TILE),
@@ -603,9 +605,10 @@
     sol_src, sol_tgt, grad_src, grad_tgt = pl.pallas_call(
         hand_out,
         out_shape=shapes,
-        in_specs=[vmem] * 4,
+        in_specs=[far] * 4,
         out_specs=[far] * 4,
-        scratch_shapes=[pltpu.SemaphoreType.DMA((4,))],
+        scratch_shapes=[buf(*shape.shape) for shape in shapes] + [pltpu.SemaphoreType.DMA((2 * (XS + 3),))],
+        compiler_params=pltpu.CompilerParams(vmem_limit_bytes=60 * 1024 * 1024),
     )(*results)
     return (
         sol_src.reshape(NS), sol_tgt.reshape(NT), grad_src.reshape(DIM, NS), grad_tgt.reshape(DIM, NT)

time: 69.4 us -> 70.9 us (1.022)
  Pallas kernels: 68.6 us -> 70 us
    pallas_call x1, Pallas kernels: 66.3 us -> 67.9 us  [body(): pl.pallas_call(functools.partial(kernel, math.log2(normalizer)), out_shap...]
where the time goes in v4:
time: 70.9 us; the launch traced here: 70.6 us
  Pallas kernels  70 us (99%)
    pallas_call x1, Pallas kernels, body(): pl.pallas_call(functools.partial(kernel, math.log2(normalizer)), out_shap...  67.9 us
    pallas_call x1, Pallas kernels, body(): pl.pallas_call(hand_out, out_shape=shapes, in_specs=[far] * 4, out_specs=...  2.08 us

profile of v4, /device:TPU:1, one launch (start us, length us, event | category | flops | bytes accessed | tf_op | source)
XLA Modules:
  0.0 70.6 jit_solution(11151298777558269379)
XLA Ops:
  0.6 67.9 %shard_map.93 = (f32[1,512]{1,0:T(1,128)}, f32[1,4096]{1,0:T(1,128)}, f32[8,8,512]{2,1,0:T(8,128)}, f32[4,16,4096]{2,1,0:T(8,128)}) custom-call(f32[2,32,512]{2,1,0:T(8,128)} %bitcast.9, f32[64,4096]{1,0:T(8,128)} %yt_hbm.1, f32[1,512]{1,0:T(1,128)} %bitcast.12, f32[1,4096]{1,0:T(1,128)} %bitcast.10, f32[1,512]{1,0:T(1,128)} %bitcast.13, f32[1,4096]{1,0:T(1,128)} %bitcast.11), custom_call_target="tpu_custom_call" | custom-call | tf_op jit(solution)/shard_map/pallas_call | solution.py:592
  68.5 2.1 %shard_map.94 = (f32[1,512]{1,0:T(1,128)}, f32[1,4096]{1,0:T(1,128)}, f32[8,8,512]{2,1,0:T(8,128)}, f32[4,16,4096]{2,1,0:T(8,128)}) custom-call(f32[1,512]{1,0:T(1,128)} %get-tuple-element.12.refs_0_, f32[1,4096]{1,0:T(1,128)} %get-tuple-element.13.refs_1_, f32[8,8,512]{2,1,0:T(8,128)} %get-tuple-element.14.refs_2_, f32[4,16,4096]{2,1,0:T(8,128)} %get-tuple-element.15.refs_3_), custom_call_target="tpu_custom_call" | custom-call | tf_op jit(solution)/shard_map/pallas_call | solution.py:605

commit v5 on v3

--- a/solution.py
+++ b/solution.py
@@ -21,6 +21,8 @@
 NS, NT = 512, 4096
 SUB = NT // SW
 TILE = 512
+STEP = 128
+ROWS = 64
 STACK = 80
 VECS = 4
 
@@ -48,6 +50,13 @@
 
 def tiled(block, times):
     return jnp.concatenate([block] * times, axis=1)
+
+
+def lane_tiles(value):
+    parts = [value[:, k:k + 128] for k in range(0, value.shape[1], 128)]
+    while len(parts) > 1:
+        parts = [parts[k] + parts[k + 1] for k in range(0, len(parts), 2)]
+    return parts[0]
 
 
 def total(value):
@@ -161,32 +170,27 @@
     loads[0].wait()
 
     def plan_step(n, carry):
-        cs = pl.ds(pl.multiple_of(n * TILE, TILE), TILE)
+        cs = pl.ds(pl.multiple_of(n * STEP, STEP), STEP)
         high, low = halves(yt_ref[:, cs])
-        y4[0:64, cs] = high
-        y4[64:128, cs] = low
-        y4[128:192, cs] = high
-        y4[192:256, cs] = low
-        cross = jnp.dot(
-            x4t[...], jnp.concatenate([high, low, high, low], axis=0), preferred_element_type=F32
-        )
+        parts = jnp.concatenate([high, low, high, low], axis=0)
+        y4[:, cs] = parts
+        cross = jnp.dot(x4t[...], parts, preferred_element_type=F32)
         g_now = g_ref[:, cs] * LOG2E
         b_now = b0_ref[:, cs]
-        mass_sum = jnp.zeros((8, TILE), F32)
-        a_sum = jnp.zeros((8, TILE), F32)
-        for r in range(0, NS, 64):
-            p = jnp.exp2(cross[r:r + 64, :] + tiled(fcol[r:r + 64, :], 4) + g_now)
-            plan[r:r + 64, cs] = p
-            racc[r:r + 64, :] += (p[:, 0:128] + p[:, 128:256]) + (p[:, 256:384] + p[:, 384:512])
-            pb = p * b_now
-            racc2[r:r + 64, :] += (pb[:, 0:128] + pb[:, 128:256]) + (pb[:, 256:384] + pb[:, 384:512])
-            pa = p * tiled(acol[r:r + 64, :], 4)
-            mass_sum = mass_sum + jnp.sum(p.reshape(8, 8, TILE), axis=0)
-            a_sum = a_sum + jnp.sum(pa.reshape(8, 8, TILE), axis=0)
+        mass_sum = jnp.zeros((8, STEP), F32)
+        a_sum = jnp.zeros((8, STEP), F32)
+        for r in range(0, NS, ROWS):
+            p = jnp.exp2(cross[r:r + ROWS, :] + tiled(fcol[r:r + ROWS, :], STEP // 128) + g_now)
+            plan[r:r + ROWS, cs] = p
+            racc[r:r + ROWS, :] += lane_tiles(p)
+            racc2[r:r + ROWS, :] += lane_tiles(p * b_now)
+            pa = p * tiled(acol[r:r + ROWS, :], STEP // 128)
+            mass_sum = mass_sum + jnp.sum(p.reshape(ROWS // 8, 8, STEP), axis=0)
+            a_sum = a_sum + jnp.sum(pa.reshape(ROWS // 8, 8, STEP), axis=0)
         col_a[0:1, cs] = jnp.sum(mass_sum, axis=0, keepdims=True)
         col_a[1:2, cs] = jnp.sum(a_sum, axis=0, keepdims=True)
         return carry
-    lax.fori_loop(0, NT // TILE, plan_step, 0)
+    lax.fori_loop(0, NT // STEP, plan_step, 0, unroll=2)
 
     mass_part = along(racc[...])
     v_part = along(racc2[...])
@@ -222,12 +226,15 @@
         zz = lax.rem(z + p, ZS)
         points = jnp.concatenate([xg[zz, 0], xg[zz, 1]], axis=0)
         fcol[...] = across(init_in[zz][0:1, :] * LOG2E + shift)
-        cross = jnp.dot(x_parts(points), y4[:, my_tile], preferred_element_type=F32)
-        for r in range(0, NS, 64):
-            value = jnp.exp2(cross[r:r + 64, :] + tiled(fcol[r:r + 64, :], 4) + g_sub)
-            high, low = halves(value)
-            q_hi[zz, r:r + 64, :] = high
-            q_lo[zz, r:r + 64, :] = low
+        parts = x_parts(points)
+        for c in range(0, TILE, 128):
+            some = pl.ds(pl.multiple_of(z * TILE + c, 128), 128)
+            cross = jnp.dot(parts, y4[:, some], preferred_element_type=F32)
+            for r in range(0, NS, 64):
+                value = jnp.exp2(cross[r:r + 64, :] + fcol[r:r + 64, :] + g_sub[:, c:c + 128])
+                high, low = halves(value)
+                q_hi[zz, r:r + 64, c:c + 128] = high
+                q_lo[zz, r:r + 64, c:c + 128] = low
         return carry
 
     def pass_on(p, k):
@@ -373,10 +380,6 @@
     row_sums(2, 3)
     col_sums(0, 3, 0, 3)
     col_sums(0, 3, 6, 8)
-    wait_in(xg.at[0, 0], G_RING4)
-    for p in (3, ZS - 3, 4):
-        zz = lax.rem(z + p, ZS)
-        push(xg.at[zz, core], xg.at[zz, core], G_SIB2, sibling)
 
     wait_in(row_b_in.at[pl.ds(0, TW - 1)], B_ROW)
     row_full1 = jnp.sum(row_b_in[...], axis=0)
@@ -390,6 +393,10 @@
     push_all(TW, tgt_peer, lambda p: sc2_out.at[0], ags_b_in.at[t], B_AGS)
     push_all(ZS, z_peer, lambda p: agz_b.at[z], agz_b.at[z], B_AGZ)
     ags_b_in[t] = sc2_out[0]
+    wait_in(xg.at[0, 0], G_RING4)
+    for p in (3, ZS - 3, 4):
+        zz = lax.rem(z + p, ZS)
+        push(xg.at[zz, core], xg.at[zz, core], G_SIB2, sibling)
     wait_in(xg.at[pl.ds(0, 3), 0], G_SIB2)
     lax.fori_loop(3, 6, q_block, 0)
     col_sums(0, 3, 3, 6)
@@ -543,13 +550,21 @@
 
 
 def hand_out(*refs):
-    count = len(refs) // 2
     sems = refs[-1]
-    copies = [pltpu.make_async_copy(refs[k], refs[count + k], sems.at[k]) for k in range(count)]
-    for copy in copies:
-        copy.start()
-    for copy in copies:
-        copy.wait()
+    parts = [(refs[3].at[k], refs[7].at[k], refs[11].at[k]) for k in range(XS)]
+    parts += [(refs[k], refs[4 + k], refs[8 + k]) for k in (2, 1, 0)]
+    loads = [pltpu.make_async_copy(src, near, sems.at[k]) for k, (src, _, near) in enumerate(parts)]
+    stores = [
+        pltpu.make_async_copy(near, dst, sems.at[len(parts) + k])
+        for k, (_, dst, near) in enumerate(parts)
+    ]
+    for load in loads:
+        load.start()
+    for load, store in zip(loads, stores):
+        load.wait()
+        store.start()
+    for store in stores:
+        store.wait()
 
 
 def body(src_points, tgt_points, src_potential, tgt_potential, src_rhs, tgt_rhs):
@@ -603,9 +618,10 @@
     sol_src, sol_tgt, grad_src, grad_tgt = pl.pallas_call(
         hand_out,
         out_shape=shapes,
-        in_specs=[vmem] * 4,
+        in_specs=[far] * 4,
         out_specs=[far] * 4,
-        scratch_shapes=[pltpu.SemaphoreType.DMA((4,))],
+        scratch_shapes=[buf(*shape.shape) for shape in shapes] + [pltpu.SemaphoreType.DMA((2 * (XS + 3),))],
+        compiler_params=pltpu.CompilerParams(vmem_limit_bytes=60 * 1024 * 1024),
     )(*results)
     return (
         sol_src.reshape(NS), sol_tgt.reshape(NT), grad_src.reshape(DIM, NS), grad_tgt.reshape(DIM, NT)

time: 69.4 us -> 71.4 us (1.029)
  Pallas kernels: 68.6 us -> 70.6 us
    pallas_call x1, Pallas kernels: 66.3 us -> 68.6 us  [body(): pl.pallas_call(functools.partial(kernel, math.log2(normalizer)), out_shap...]
where the time goes in v5:
time: 71.4 us; the launch traced here: 71.3 us
  Pallas kernels  70.6 us (99%)
    pallas_call x1, Pallas kernels, body(): pl.pallas_call(functools.partial(kernel, math.log2(normalizer)), out_shap...  68.6 us
    pallas_call x1, Pallas kernels, body(): pl.pallas_call(hand_out, out_shape=shapes, in_specs=[far] * 4, out_specs=...  2.08 us

profile of v5, /device:TPU:1, one launch (start us, length us, event | category | flops | bytes accessed | tf_op | source)
XLA Modules:
  0.0 71.3 jit_solution(4376146881392433235)
XLA Ops:
  0.6 68.6 %shard_map.93 = (f32[1,512]{1,0:T(1,128)}, f32[1,4096]{1,0:T(1,128)}, f32[8,8,512]{2,1,0:T(8,128)}, f32[4,16,4096]{2,1,0:T(8,128)}) custom-call(f32[2,32,512]{2,1,0:T(8,128)} %bitcast.9, f32[64,4096]{1,0:T(8,128)} %yt_hbm.1, f32[1,512]{1,0:T(1,128)} %bitcast.12, f32[1,4096]{1,0:T(1,128)} %bitcast.10, f32[1,512]{1,0:T(1,128)} %bitcast.13, f32[1,4096]{1,0:T(1,128)} %bitcast.11), custom_call_target="tpu_custom_call" | custom-call | tf_op jit(solution)/shard_map/pallas_call | solution.py:605
  69.2 2.1 %shard_map.94 = (f32[1,512]{1,0:T(1,128)}, f32[1,4096]{1,0:T(1,128)}, f32[8,8,512]{2,1,0:T(8,128)}, f32[4,16,4096]{2,1,0:T(8,128)}) custom-call(f32[1,512]{1,0:T(1,128)} %get-tuple-element.12.refs_0_, f32[1,4096]{1,0:T(1,128)} %get-tuple-element.13.refs_1_, f32[8,8,512]{2,1,0:T(8,128)} %get-tuple-element.14.refs_2_, f32[4,16,4096]{2,1,0:T(8,128)} %get-tuple-element.15.refs_3_), custom_call_target="tpu_custom_call" | custom-call | tf_op jit(solution)/shard_map/pallas_call | solution.py:618

commit v6 on v5

--- a/solution.py
+++ b/solution.py
@@ -21,7 +21,7 @@
 NS, NT = 512, 4096
 SUB = NT // SW
 TILE = 512
-STEP = 128
+STEP = 256
 ROWS = 64
 STACK = 80
 VECS = 4
@@ -190,7 +190,7 @@
         col_a[0:1, cs] = jnp.sum(mass_sum, axis=0, keepdims=True)
         col_a[1:2, cs] = jnp.sum(a_sum, axis=0, keepdims=True)
         return carry
-    lax.fori_loop(0, NT // STEP, plan_step, 0, unroll=2)
+    lax.fori_loop(0, NT // STEP, plan_step, 0)
 
     mass_part = along(racc[...])
     v_part = along(racc2[...])
@@ -226,15 +226,12 @@
         zz = lax.rem(z + p, ZS)
         points = jnp.concatenate([xg[zz, 0], xg[zz, 1]], axis=0)
         fcol[...] = across(init_in[zz][0:1, :] * LOG2E + shift)
-        parts = x_parts(points)
-        for c in range(0, TILE, 128):
-            some = pl.ds(pl.multiple_of(z * TILE + c, 128), 128)
-            cross = jnp.dot(parts, y4[:, some], preferred_element_type=F32)
-            for r in range(0, NS, 64):
-                value = jnp.exp2(cross[r:r + 64, :] + fcol[r:r + 64, :] + g_sub[:, c:c + 128])
-                high, low = halves(value)
-                q_hi[zz, r:r + 64, c:c + 128] = high
-                q_lo[zz, r:r + 64, c:c + 128] = low
+        cross = jnp.dot(x_parts(points), y4[:, my_tile], preferred_element_type=F32)
+        for r in range(0, NS, 64):
+            value = jnp.exp2(cross[r:r + 64, :] + tiled(fcol[r:r + 64, :], 4) + g_sub)
+            high, low = halves(value)
+            q_hi[zz, r:r + 64, :] = high
+            q_lo[zz, r:r + 64, :] = low
         return carry
 
     def pass_on(p, k):

time: 71.4 us -> 70.5 us (0.987)
  Pallas kernels: 70.6 us -> 69.8 us
    pallas_call x1, Pallas kernels: 68.6 us -> 67.7 us  [body(): pl.pallas_call(functools.partial(kernel, math.log2(normalizer)), out_shap...]
where the time goes in v6:
time: 70.5 us; the launch traced here: 70.4 us
  Pallas kernels  69.8 us (99%)
    pallas_call x1, Pallas kernels, body(): pl.pallas_call(functools.partial(kernel, math.log2(normalizer)), out_shap...  67.7 us
    pallas_call x1, Pallas kernels, body(): pl.pallas_call(hand_out, out_shape=shapes, in_specs=[far] * 4, out_specs=...  2.08 us

profile of v6, /device:TPU:1, one launch (start us, length us, event | category | flops | bytes accessed | tf_op | source)
XLA Modules:
  0.0 70.4 jit_solution(9499223344707434808)
XLA Ops:
  0.6 67.7 %shard_map.93 = (f32[1,512]{1,0:T(1,128)}, f32[1,4096]{1,0:T(1,128)}, f32[8,8,512]{2,1,0:T(8,128)}, f32[4,16,4096]{2,1,0:T(8,128)}) custom-call(f32[2,32,512]{2,1,0:T(8,128)} %bitcast.9, f32[64,4096]{1,0:T(8,128)} %yt_hbm.1, f32[1,512]{1,0:T(1,128)} %bitcast.12, f32[1,4096]{1,0:T(1,128)} %bitcast.10, f32[1,512]{1,0:T(1,128)} %bitcast.13, f32[1,4096]{1,0:T(1,128)} %bitcast.11), custom_call_target="tpu_custom_call" | custom-call | tf_op jit(solution)/shard_map/pallas_call | solution.py:602
  68.3 2.1 %shard_map.94 = (f32[1,512]{1,0:T(1,128)}, f32[1,4096]{1,0:T(1,128)}, f32[8,8,512]{2,1,0:T(8,128)}, f32[4,16,4096]{2,1,0:T(8,128)}) custom-call(f32[1,512]{1,0:T(1,128)} %get-tuple-element.12.refs_0_, f32[1,4096]{1,0:T(1,128)} %get-tuple-element.13.refs_1_, f32[8,8,512]{2,1,0:T(8,128)} %get-tuple-element.14.refs_2_, f32[4,16,4096]{2,1,0:T(8,128)} %get-tuple-element.15.refs_3_), custom_call_target="tpu_custom_call" | custom-call | tf_op jit(solution)/shard_map/pallas_call | solution.py:615
